TPU v7x, 32 devices: a whole 2x2x4 slice. The times are simulated.
32 devices in a mesh: lon: 2 (over y), lat: 16 (over z, x, core).
Axes of the slice: x: 2, y: 2, z: 4, core: 2. Of those that a mesh axis runs over, the one named last changes fastest.
Arguments:
- state: float32 [5, 32, 192, 2880], P(None, None, 'lat', 'lon'), may hold values from -6 to 6
- decay: float32 [32, 192, 2880], P(None, 'lat', 'lon'), may hold values from 0.48 to 1, as said below
- band_rows: int32 [64], replicated, may hold values from 0 to 191, as said below
Outputs:
- advanced: float32 [5, 32, 192, 2880], P(None, None, 'lat', 'lon')
Inputs may be any that keep to these rules, and one draw needn't show every extreme that they name: `band_rows`: the first m rows of the grid and the last 64 - m rows, for some m from 16 to 48. `decay`: every entry is at most 1 - 1 / 5760, so the product over a row's 2880 columns is at most exp(-1/2).
All inputs are finite; a program needn't handle non-finite values.
Results may differ from a plain program's by a relative error of at most 0.0003.
Values sent between devices are 32-bit elements; how exact they have to be, the bound alone decides.
A program may use at most 384 MiB of HBM per device.

v0:
```python
import jax
import jax.numpy as jnp
from jax import lax
from jax.sharding import PartitionSpec as P

SUBSTEPS = 2


time_step = 0.2
coriolis = 0.5
edge_cosine = 0.5


def prefix(x, axis, combine, identity):
    devices, mine = (lax.axis_size(axis), lax.axis_index(axis))
    everything = jax.tree.map(lambda part: lax.all_gather(part, axis), x)
    start = jax.tree.map(
        lambda part, zero: jnp.broadcast_to(jnp.asarray(zero, part.dtype), part.shape), x, identity
    )

    def turn(k, before):
        reached = k < mine
        new = combine(before, jax.tree.map(lambda part: part[k], everything))
        return jax.tree.map(lambda a, b: jnp.where(reached, a, b), new, before)

    return lax.fori_loop(0, devices, turn, start)


def spread(block, axis, source):
    block = jnp.where(lax.axis_index(axis) == source, block, jnp.zeros_like(block))
    return lax.psum(block, axis)


def extended(cells, sides, width, closed):
    for axis, dim in sides:
        count = lax.axis_size(axis)
        ends = count if closed else count - 1
        head = lax.slice_in_dim(cells, 0, width, axis=dim)
        tail = lax.slice_in_dim(cells, cells.shape[dim] - width, cells.shape[dim], axis=dim)
        cells = jnp.concatenate(
            [
                lax.ppermute(tail, axis, [(i, (i + 1) % count) for i in range(ends)]),
                cells,
                lax.ppermute(head, axis, [((i + 1) % count, i) for i in range(ends)]),
            ],
            axis=dim,
        )
    return cells


def angles(index, count):
    return jnp.pi * index.astype(jnp.float32) / count


def faces_of(padded, axis):
    length = padded.shape[axis] - 4

    def portion(begin):
        return lax.slice_in_dim(padded, begin, begin + length + 1, axis=axis)

    return (7.0 * (portion(1) + portion(2)) - (portion(0) + portion(3))) / 12.0


def slope_of(padded, axis):
    length = padded.shape[axis] - 4

    def portion(begin):
        return lax.slice_in_dim(padded, begin, begin + length, axis=axis)

    return (8.0 * (portion(3) - portion(1)) - (portion(4) - portion(0))) / 12.0


def difference(faces, axis):
    length = faces.shape[axis] - 1
    return lax.slice_in_dim(faces, 1, length + 1, axis=axis) - lax.slice_in_dim(
        faces, 0, length, axis=axis
    )


def tendency(lon_padded, lat_padded, cosine, sine, face_cos):

    def advect(index):
        zonal_part = difference(faces_of(lon_padded[index] * lon_padded[1], -1), -1)
        merid_part = difference(face_cos * faces_of(lat_padded[index] * lat_padded[2], -2), -2)
        return -(zonal_part + merid_part) / cosine

    zonal_wind = lat_padded[1][..., 2:-2, :]
    merid_wind = lat_padded[2][..., 2:-2, :]
    zonal_force = -slope_of(lon_padded[0], -1) / cosine + coriolis * sine * merid_wind
    merid_force = -slope_of(lat_padded[0], -2) - coriolis * sine * zonal_wind
    return jnp.stack([advect(0), zonal_force, merid_force, advect(3), advect(4)])


def compose(earlier, later):
    return (earlier[0] * later[0], later[0] * earlier[1] + later[1])


def entry_value(pre_scale, pre_offset, total_scale, total_offset):
    start_value = total_offset / (1.0 - total_scale)
    return pre_scale * start_value + pre_offset


def inflow_of(own_scale, own_offset):
    pre_scale, pre_offset = prefix(
        (own_scale, own_offset),
        "lon",
        compose,
        (jnp.ones_like(own_scale), jnp.zeros_like(own_offset)),
    )
    whole_scale, whole_offset = compose((pre_scale, pre_offset), (own_scale, own_offset))
    joined = spread(
        jnp.concatenate([whole_scale, whole_offset], axis=0), "lon", lax.axis_size("lon") - 1
    )
    total_scale = joined[:1]
    total_offset = joined[1:]
    return entry_value(pre_scale, pre_offset, total_scale, total_offset)


def shifted_by(values, stride, fill):
    widths = [(0, 0)] * (values.ndim - 1) + [(stride, 0)]
    return jnp.pad(values[..., :-stride], widths, constant_values=fill)


def local_maps(values, rates_table):
    gain = jnp.sqrt(1.0 - rates_table * rates_table)
    scale = rates_table[None]
    offset = gain[None] * values
    width = values.shape[-1]
    stride = 1
    while stride < width:
        offset = scale * shifted_by(offset, stride, 0.0) + offset
        scale = scale * shifted_by(scale, stride, 1.0)
        stride = stride * 2
    return (scale, offset)


def cyclic(values, rates_table):
    scale, offset = local_maps(values, rates_table)
    inflow = inflow_of(scale[..., -1], offset[..., -1])
    return offset + scale * inflow[..., None]


def per_device(state, decay, band_rows):
    local_rows = state.shape[2]
    local_cols = state.shape[3]
    lat_count = lax.axis_size("lat")
    total_rows = local_rows * lat_count
    total_cols = local_cols * lax.axis_size("lon")
    lat_index = lax.axis_index("lat")
    is_south = lat_index == 0
    is_north = lat_index == lat_count - 1
    rows = lat_index * local_rows + jnp.arange(local_rows, dtype=jnp.int32)
    centre = angles(2 * rows + 1, 2 * total_rows)
    cosine = jnp.sin(centre)[:, None]
    sine = -jnp.cos(centre)[:, None]
    face_rows = lat_index * local_rows + jnp.arange(local_rows + 1, dtype=jnp.int32)
    face_cos = jnp.sin(angles(face_rows, total_rows))[:, None]
    in_band = jnp.any(rows[:, None] == band_rows[None, :], axis=1)
    for substep in range(SUBSTEPS):
        lon_padded = extended(state, (("lon", 3),), 2, True)
        lat_padded = extended(state, (("lat", 2),), 2, False)
        rates = tendency(lon_padded, lat_padded, cosine, sine, face_cos)
        south_sum = jnp.sum(rates[:, :, 0, :], axis=-1)
        north_sum = jnp.sum(rates[:, :, -1, :], axis=-1)
        picked = rates
        southern = (rows < total_rows // 2)[None, None, :, None]
        row_cos = jnp.sin(angles(2 * rows + 1, 2 * total_rows))[:, None]
        south_cycle, north_cycle = lax.psum((south_sum, north_sum), "lon")
        south_cap = jnp.where(is_south, south_cycle, 0.0)
        north_cap = jnp.where(is_north, north_cycle, 0.0)
        south_total, north_total = lax.psum((south_cap, north_cap), "lat")
        panel = jnp.where(
            southern,
            (south_total / total_cols)[:, :, None, None],
            (north_total / total_cols)[:, :, None, None],
        )
        smoothed = panel + row_cos / edge_cosine * cyclic(picked - panel, decay)
        rates = jnp.where(in_band[None, None, :, None], smoothed, rates)
        state = state + time_step * rates
    return state


def solution(mesh):
    placed = (P(None, None, "lat", "lon"), P(None, "lat", "lon"), P())
    return jax.shard_map(
        per_device,
        mesh=mesh,
        in_specs=placed,
        out_specs=P(None, None, "lat", "lon"),
        check_vma=False,
    )
```

profile of v0, /device:TPU:0, one launch (start us, length us, event | category | flops | bytes accessed | tf_op | source)
XLA Modules:
  0.0 846.5 jit_solution(17433833676877790795)
XLA Ops:
  22.0 8.3 copy.310
  30.4 10.7 %slice.731 = f32[1,32,12,1439]{1,2,3,0:T(8,128)} slice(f32[1,32,12,1440]{1,2,3,0:T(8,128)} %bitcast.213), slice={[0:1], [0:32], [0:12], [0:1439]} | slice | bytes 4420608 | tf_op jit(solution)/shard_map/slice | solution.py:121
  83.0 6.3 pad_multiply_fusion.7
  155.5 6.7 pad_multiply_fusion.1
  171.6 8.9 %copy.320 = f32[32,12,1440]{2,0,1:T(8,128)} copy(f32[32,12,1440]{0,1,2:T(8,128)} %bitcast.195) | data formatting | bytes 4423680 | tf_op jit(solution)/shard_map/mul | solution.py:131
  180.5 8.9 %copy.319 = f32[32,12,1440]{2,0,1:T(8,128)} copy(f32[32,12,1440]{0,1,2:T(8,128)} %bitcast.196) | data formatting | bytes 4423680 | tf_op jit(solution)/shard_map/mul | solution.py:131
  189.4 8.9 %copy.318 = f32[32,12,1440]{2,0,1:T(8,128)} copy(f32[32,12,1440]{0,1,2:T(8,128)} %bitcast.197) | data formatting | bytes 4423680 | tf_op jit(solution)/shard_map/mul | solution.py:131
  198.3 8.9 %copy.317 = f32[32,12,1440]{2,0,1:T(8,128)} copy(f32[32,12,1440]{0,1,2:T(8,128)} %bitcast.198) | data formatting | bytes 4423680 | tf_op jit(solution)/shard_map/mul | solution.py:131
  207.2 8.9 %copy.316 = f32[32,12,1440]{2,0,1:T(8,128)} copy(f32[32,12,1440]{0,1,2:T(8,128)} %bitcast.199) | data formatting | bytes 4423680 | tf_op jit(solution)/shard_map/mul | solution.py:131
  216.1 8.9 %copy.315 = f32[32,12,1440]{2,0,1:T(8,128)} copy(f32[32,12,1440]{0,1,2:T(8,128)} %bitcast.200) | data formatting | bytes 4423680 | tf_op jit(solution)/shard_map/mul | solution.py:131
  225.0 8.9 %copy.314 = f32[32,12,1440]{2,0,1:T(8,128)} copy(f32[32,12,1440]{0,1,2:T(8,128)} %bitcast.201) | data formatting | bytes 4423680 | tf_op jit(solution)/shard_map/mul | solution.py:131
  233.9 8.9 %copy.313 = f32[32,12,1440]{2,0,1:T(8,128)} copy(f32[32,12,1440]{0,1,2:T(8,128)} %bitcast.202) | data formatting | bytes 4423680 | tf_op jit(solution)/shard_map/mul | solution.py:131
  242.8 8.9 %copy.312 = f32[32,12,1440]{2,0,1:T(8,128)} copy(f32[32,12,1440]{0,1,2:T(8,128)} %bitcast.203) | data formatting | bytes 4423680 | tf_op jit(solution)/shard_map/mul | solution.py:131
  251.7 8.9 %copy.311 = f32[32,12,1440]{2,0,1:T(8,128)} copy(f32[32,12,1440]{0,1,2:T(8,128)} %bitcast.204) | data formatting | bytes 4423680 | tf_op jit(solution)/shard_map/mul | solution.py:131
  265.6 9.3 %copy.321 = f32[32,12,1440]{2,0,1:T(8,128)} copy(f32[32,12,1440]{0,1,2:T(8,128)} %bitcast.214) | data formatting | bytes 4423680 | tf_op jit(solution)/shard_map/mul | solution.py:140
  277.4 15.1 %concatenate.18 = f32[5,32,12,1444]{3,1,2,0:T(8,128)} concatenate(f32[5,32,12,2]{3,1,2,0:T(8,128)S(1)} %copy.308, f32[5,32,12,1440]{3,1,2,0:T(8,128)} %param.7, f32[5,32,12,2]{3,1,2,0:T(8,128)S(1)} %copy.309), dimensions={3} | concatenate | bytes 22179840 | tf_op jit(solution)/shard_map/concatenate | solution.py:40
  310.7 10.7 %constant_dynamic-update-slice_fusion.1 = f32[5,32,16,1440]{3,1,2,0:T(8,128)} fusion(f32[5,32,16,1440]{3,1,2,0:T(8,128)} %constant_dynamic-update-slice_fusion.2, f32[5,32,12,1440]{3,1,2,0:T(8,128)} %param.7), kind=kLoop, calls=%fused_computation.238 | loop fusion | bytes 23592960
  324.4 6.2 fusion.4
  330.6 7.8 slice_bitcast_fusion.9
  366.4 31.8 %all-reduce.34 = (f32[5,32]{1,0:T(8,128)S(1)}, f32[5,32]{1,0:T(8,128)S(1)}) all-reduce(f32[5,32]{1,0:T(8,128)S(1)} %broadcast_select_fusion.8, f32[5,32]{1,0:T(8,128)S(1)} %broadcast_select_fusion.9), channel_id=1, replica_groups=mesh['lon'=2,'lat'=16] {'lat'}, use_global_device_ids=true, to_apply=%region_6.7 | all-reduce | flops 320 | bytes 2560 | tf_op jit(solution)/shard_map/psum | solution.py:171
  398.3 9.7 %subtract_multiply_fusion.1 = f32[5,32,12,1440]{3,1,2,0:T(8,128)} fusion(f32[5,32,12,1440]{3,1,2,0:T(8,128)} %copy-done.9, f32[32,12,1440]{2,0,1:T(8,128)S(1)} %copy-done.13, f32[5,32,12]{1,2,0:T(8,128)S(1)} %broadcast_select_fusion.5), kind=kLoop, calls=%fused_computation.39 | loop fusion | flops 5529600 | bytes 24337920 | tf_op jit(solution)/shard_map/mul | solution.py:127
  408.1 10.4 %multiply_add_fusion.23 = f32[5,32,12,1440]{3,1,2,0:T(8,128)S(1)} fusion(f32[5,32,12,1439]{3,1,2,0:T(8,128)} %bitcast.216, f32[32,12,1440]{2,0,1:T(8,128)} %param.8, f32[5,32,12,1440]{3,1,2,0:T(8,128)} %copy-done.9, f32[5,32,12]{1,2,0:T(8,128)S(1)} %broadcast_select_fusion.5, f32[32,12,1440]{2,0,1:T(8,128)S(1)} %copy-done.13), kind=kLoop, calls=%fused_computation.38 | loop fusion | flops 11059200 | bytes 37601280 | tf_op jit(solution)/shard_map/add | solution.py:131
  432.6 6.4 multiply_add_fusion.19
  439.1 9.2 %slice.746 = f32[5,32,12,1408]{3,1,2,0:T(8,128)} slice(f32[5,32,12,1440]{3,1,2,0:T(8,128)} %multiply_add_fusion.19), slice={[0:5], [0:32], [0:12], [0:1408]} | slice | bytes 21626880 | tf_op jit(solution)/shard_map/slice | solution.py:121
  448.2 9.4 %multiply_add_fusion.18 = f32[5,32,12,1440]{3,1,2,0:T(8,128)S(1)} fusion(f32[5,32,12,1440]{3,1,2,0:T(8,128)} %multiply_add_fusion.19, f32[5,32,12,1408]{3,1,2,0:T(8,128)} %slice.746, f32[32,12,1440]{2,0,1:T(8,128)} %copy.316), kind=kLoop, calls=%fused_computation.33 | loop fusion | flops 5529600 | bytes 35143680 | tf_op jit(solution)/shard_map/add | solution.py:131
  463.1 11.4 %multiply_add_fusion.17 = f32[5,32,12,1440]{3,1,2,0:T(8,128)} fusion(f32[5,32,12,1440]{3,1,2,0:T(8,128)S(1)} %multiply_add_fusion.18, f32[5,32,12,1376]{3,1,2,0:T(8,128)} %slice.747, f32[32,12,1440]{2,0,1:T(8,128)} %copy.315), kind=kLoop, calls=%fused_computation.32 | loop fusion | flops 5529600 | bytes 34897920 | tf_op jit(solution)/shard_map/add | solution.py:131
  478.5 11.2 %multiply_add_fusion.16 = f32[5,32,12,1440]{3,1,2,0:T(8,128)} fusion(f32[5,32,12,1440]{3,1,2,0:T(8,128)} %multiply_add_fusion.17, f32[5,32,12,1312]{3,1,2,0:T(8,128)S(1)} %slice-done.5, f32[32,12,1440]{2,0,1:T(8,128)} %copy.314), kind=kLoop, calls=%fused_computation.31 | loop fusion | flops 5529600 | bytes 34406400 | tf_op jit(solution)/shard_map/add | solution.py:131
  494.3 10.7 %multiply_add_fusion.15 = f32[5,32,12,1440]{3,1,2,0:T(8,128)} fusion(f32[5,32,12,1440]{3,1,2,0:T(8,128)} %multiply_add_fusion.16, f32[5,32,12,1184]{3,1,2,0:T(8,128)S(1)} %slice-done.7, f32[32,12,1440]{2,0,1:T(8,128)S(1)} %copy-done.25), kind=kLoop, calls=%fused_computation.30 | loop fusion | flops 5529600 | bytes 33423360 | tf_op jit(solution)/shard_map/add | solution.py:131
  508.9 6.2 multiply_add_fusion.14
  532.3 8.5 psum.74
  540.9 12.4 %multiply_add_fusion.12 = f32[5,32,12,1440]{3,1,2,0:T(8,128)S(1)} fusion(f32[5,32,12,1440]{3,1,2,0:T(8,128)} %param.7, f32[5,32,12,1440]{3,1,2,0:T(8,128)} %copy-done.9, f32[5,32,12,1440]{3,1,2,0:T(8,128)} %copy-done.16, f32[5,32,12]{1,2,0:T(8,128)S(1)} %fusion.111, f32[32,12,1440]{2,0,1:T(8,128)S(1)} %copy-done.19, f32[12]{0:T(128)S(1)} %copy-done.55, ...), kind=kLoop, calls=%fused_computation.26 | loop fusion | flops 19353600 | bytes 46464060 | tf_op jit(solution)/shard_map/add | solution.py:179
  570.3 15.1 %concatenate.21 = f32[5,32,12,1444]{3,1,2,0:T(8,128)} concatenate(f32[5,32,12,2]{3,1,2,0:T(8,128)S(1)} %copy.328, f32[5,32,12,1440]{3,1,2,0:T(8,128)} %copy-done, f32[5,32,12,2]{3,1,2,0:T(8,128)S(1)} %copy.329), dimensions={3} | concatenate | bytes 22179840 | tf_op jit(solution)/shard_map/concatenate | solution.py:40
  602.0 7.7 pad_maximum_fusion
  609.7 6.8 fusion.2
  616.6 7.7 slice_bitcast_fusion.4
  624.3 6.8 fusion.7
  653.1 34.4 %all-reduce.33 = (f32[5,32]{1,0:T(8,128)S(1)}, f32[5,32]{1,0:T(8,128)S(1)}) all-reduce(f32[5,32]{1,0:T(8,128)S(1)} %broadcast_select_fusion.6, f32[5,32]{1,0:T(8,128)S(1)} %broadcast_select_fusion.7), channel_id=1, replica_groups=mesh['lon'=2,'lat'=16] {'lat'}, use_global_device_ids=true, to_apply=%region_15.16 | all-reduce | flops 320 | bytes 2560 | tf_op jit(solution)/shard_map/psum | solution.py:171
  687.6 9.7 %subtract_multiply_fusion = f32[5,32,12,1440]{3,1,2,0:T(8,128)} fusion(f32[5,32,12,1440]{3,1,2,0:T(8,128)} %copy-done.10, f32[5,32,12]{1,2,0:T(8,128)S(1)} %broadcast_select_fusion.4, f32[32,12,1440]{2,0,1:T(8,128)S(1)} %copy-done.14), kind=kLoop, calls=%fused_computation.25 | loop fusion | flops 5529600 | bytes 24337920 | tf_op jit(solution)/shard_map/mul | solution.py:127
  697.3 10.1 %multiply_add_fusion.11 = f32[5,32,12,1440]{3,1,2,0:T(8,128)S(1)} fusion(f32[5,32,12,1439]{3,1,2,0:T(8,128)} %bitcast.215, f32[32,12,1440]{2,0,1:T(8,128)} %param.8, f32[5,32,12,1440]{3,1,2,0:T(8,128)} %copy-done.10, f32[5,32,12]{1,2,0:T(8,128)S(1)} %broadcast_select_fusion.4, f32[32,12,1440]{2,0,1:T(8,128)S(1)} %copy-done.14), kind=kLoop, calls=%fused_computation.24 | loop fusion | flops 11059200 | bytes 37601280 | tf_op jit(solution)/shard_map/add | solution.py:131
  721.7 6.4 multiply_add_fusion.7
  728.1 9.2 %slice.823 = f32[5,32,12,1408]{3,1,2,0:T(8,128)} slice(f32[5,32,12,1440]{3,1,2,0:T(8,128)} %multiply_add_fusion.7), slice={[0:5], [0:32], [0:12], [0:1408]} | slice | bytes 21626880 | tf_op jit(solution)/shard_map/slice | solution.py:121
  737.2 9.4 %multiply_add_fusion.6 = f32[5,32,12,1440]{3,1,2,0:T(8,128)S(1)} fusion(f32[5,32,12,1440]{3,1,2,0:T(8,128)} %multiply_add_fusion.7, f32[5,32,12,1408]{3,1,2,0:T(8,128)} %slice.823, f32[32,12,1440]{2,0,1:T(8,128)} %copy.316), kind=kLoop, calls=%fused_computation.19 | loop fusion | flops 5529600 | bytes 35143680 | tf_op jit(solution)/shard_map/add | solution.py:131
  752.2 11.3 %multiply_add_fusion.5 = f32[5,32,12,1440]{3,1,2,0:T(8,128)} fusion(f32[5,32,12,1440]{3,1,2,0:T(8,128)S(1)} %multiply_add_fusion.6, f32[5,32,12,1376]{3,1,2,0:T(8,128)} %slice.824, f32[32,12,1440]{2,0,1:T(8,128)} %copy.315), kind=kLoop, calls=%fused_computation.18 | loop fusion | flops 5529600 | bytes 34897920 | tf_op jit(solution)/shard_map/add | solution.py:131
  767.6 11.2 %multiply_add_fusion.4 = f32[5,32,12,1440]{3,1,2,0:T(8,128)} fusion(f32[5,32,12,1440]{3,1,2,0:T(8,128)} %multiply_add_fusion.5, f32[5,32,12,1312]{3,1,2,0:T(8,128)S(1)} %slice-done.4, f32[32,12,1440]{2,0,1:T(8,128)} %copy.314), kind=kLoop, calls=%fused_computation.17 | loop fusion | flops 5529600 | bytes 34406400 | tf_op jit(solution)/shard_map/add | solution.py:131
  783.3 10.7 %multiply_add_fusion.3 = f32[5,32,12,1440]{3,1,2,0:T(8,128)} fusion(f32[5,32,12,1440]{3,1,2,0:T(8,128)} %multiply_add_fusion.4, f32[5,32,12,1184]{3,1,2,0:T(8,128)S(1)} %slice-done.6, f32[32,12,1440]{2,0,1:T(8,128)S(1)} %copy-done.26), kind=kLoop, calls=%fused_computation.16 | loop fusion | flops 5529600 | bytes 33423360 | tf_op jit(solution)/shard_map/add | solution.py:131
  797.9 6.2 multiply_add_fusion.2
  821.3 7.8 psum.79
  829.2 17.1 %multiply_add_fusion = f32[5,32,12,1440]{3,1,2,0:T(8,128)} fusion(f32[5,32,12,1440]{3,1,2,0:T(8,128)} %copy-done, f32[5,32,12,1440]{3,1,2,0:T(8,128)} %copy-done.10, f32[5,32,12,1440]{3,1,2,0:T(8,128)} %copy-done.15, f32[5,32,12]{1,2,0:T(8,128)S(1)} %fusion.109, f32[5,32,12]{1,2,0:T(8,128)S(1)} %broadcast_select_fusion.4, f32[32,12,1440]{2,0,1:T(8,128)S(1)} %copy-done.20, ...), kind=kLoop, calls=%fused_computation.13 | loop fusion | flops 19353600 | bytes 46464060 | tf_op jit(solution)/shard_map/add | solution.py:179
  (293 shorter events, 350.0 us)
Async XLA Ops:
  2.9 273.2 %collective-permute-start = (f32[5,32,12,2]{1,3,2,0:T(2,128)}, f32[5,32,12,2]{1,3,2,0:T(2,128)}, u32[]{:S(2)}, u32[]{:S(2)}) collective-permute-start(f32[5,32,12,2]{1,3,2,0:T(2,128)} %copy.339), channel_id=1, source_target_pairs={{0,16},{16,0},{1,17},{17,1},{2,18},{18,2},{3,19},{19,3},{4,20},{20... | collective-permute-start | bytes 46088 | tf_op jit(solution)/shard_map/ppermute | solution.py:42
  6.9 13.1 %copy-start.18 = (f32[32,12,1440]{2,0,1:T(8,128)S(1)}, f32[32,12,1440]{2,0,1:T(8,128)}, u32[]{:S(2)}) copy-start(f32[32,12,1440]{2,0,1:T(8,128)} %param.8) | copy-start | bytes 6635524
  6.9 268.0 %collective-permute-start.1 = (f32[5,32,12,2]{1,3,2,0:T(2,128)}, f32[5,32,12,2]{1,3,2,0:T(2,128)}, u32[]{:S(2)}, u32[]{:S(2)}) collective-permute-start(f32[5,32,12,2]{1,3,2,0:T(2,128)} %copy.340), channel_id=1, source_target_pairs={{16,0},{0,16},{17,1},{1,17},{18,2},{2,18},{19,3},{3,19},{20,4},{4,... | collective-permute-start | bytes 46088 | tf_op jit(solution)/shard_map/ppermute | solution.py:44
  11.6 309.8 %collective-permute-start.3 = (f32[5,32,2,1440]{3,1,2,0:T(8,128)}, f32[5,32,2,1440]{3,1,2,0:T(8,128)}, u32[]{:S(2)}, u32[]{:S(2)}) collective-permute-start(f32[5,32,2,1440]{3,1,2,0:T(8,128)} %get-tuple-element.461), channel_id=1, source_target_pairs={{1,0},{2,1},{3,2},{4,3},{5,4},{6,5},{7,6},{8,7},{9,8},{10,9},{11,1... | collective-permute-start | bytes 5529608 | tf_op jit(solution)/shard_map/ppermute | solution.py:44
  12.9 294.8 %collective-permute-start.2 = (f32[5,32,2,1440]{3,1,2,0:T(8,128)}, f32[5,32,2,1440]{3,1,2,0:T(8,128)}, u32[]{:S(2)}, u32[]{:S(2)}) collective-permute-start(f32[5,32,2,1440]{3,1,2,0:T(8,128)} %get-tuple-element.462), channel_id=1, source_target_pairs={{0,1},{1,2},{2,3},{3,4},{4,5},{5,6},{6,7},{7,8},{8,9},{9,10},{10,1... | collective-permute-start | bytes 5529608 | tf_op jit(solution)/shard_map/ppermute | solution.py:42
  30.4 12.0 %copy-start.12 = (f32[32,12,1440]{0,1,2:T(8,128)S(1)}, f32[32,12,1440]{0,1,2:T(8,128)}, u32[]{:S(2)}) copy-start(f32[32,12,1440]{0,1,2:T(8,128)} %copy.310) | copy-start | bytes 6635524
  48.3 8.1 copy-start.1
  61.8 7.9 copy-start.2
  75.1 7.9 copy-start.3
  89.3 7.8 copy-start.4
  102.5 7.8 copy-start.5
  115.8 7.6 copy-start.6
  129.2 7.5 copy-start.7
  162.4 8.3 copy-start.63
  162.5 8.3 copy-start.64
  171.5 166.9 %copy-start.61 = (f32[13]{0:T(128)}, f32[13]{0:T(128)S(1)}, u32[]{:S(2)}) copy-start(f32[13]{0:T(128)S(1)} %sine_multiply_fusion) | copy-start | bytes 160
  338.4 5.9 copy-start.51
  344.3 4.8 copy-start.40
  344.3 4.8 copy-start.53
  355.9 42.3 %copy-start.59 = (pred[12]{0:T(512)(128)(4,1)S(1)}, pred[12]{0:T(512)(128)(4,1)}, u32[]{:S(2)}) copy-start(pred[12]{0:T(512)(128)(4,1)} %broadcast_compare_fusion) | copy-start | bytes 40
  355.9 42.4 %copy-start.13 = (f32[32,12,1440]{2,0,1:T(8,128)S(1)}, f32[32,12,1440]{2,0,1:T(8,128)}, u32[]{:S(2)}) copy-start(f32[32,12,1440]{2,0,1:T(8,128)} %subtract_sqrt_fusion) | copy-start | bytes 6635524
  423.5 5.2 copy-start.29
  525.8 5.6 copy-start.44
  525.8 5.6 copy-start.45
  525.8 5.7 copy-start.48
  525.8 6.5 copy-start.49
  525.8 15.1 %copy-start.19 = (f32[32,12,1440]{2,0,1:T(8,128)S(1)}, f32[32,12,1440]{2,0,1:T(8,128)}, u32[]{:S(2)}) copy-start(f32[32,12,1440]{2,0,1:T(8,128)} %copy.321) | copy-start | bytes 6635524
  525.8 15.1 %copy-start.55 = (f32[12]{0:T(128)S(1)}, f32[12]{0:T(128)}, u32[]{:S(2)}) copy-start(f32[12]{0:T(128)} %broadcast_multiply_fusion.4) | copy-start | bytes 148
  525.8 15.1 %copy-start.57 = (pred[12]{0:T(512)(128)(4,1)S(1)}, pred[12]{0:T(512)(128)(4,1)}, u32[]{:S(2)}) copy-start(pred[12]{0:T(512)(128)(4,1)} %compare_reduce_fusion) | copy-start | bytes 40
  559.1 10.8 %collective-permute-start.4 = (f32[5,32,12,2]{1,3,2,0:T(2,128)S(1)}, f32[5,32,12,2]{1,3,2,0:T(2,128)S(1)}, u32[]{:S(2)}, u32[]{:S(2)}) collective-permute-start(f32[5,32,12,2]{1,3,2,0:T(2,128)S(1)} %copy.326), channel_id=1, source_target_pairs={{0,16},{16,0},{1,17},{17,1},{2,18},{18,2},{3,19},{19,3},{4,20},{20... | collective-permute-start | bytes 46088 | tf_op jit(solution)/shard_map/ppermute | solution.py:42
  559.8 9.6 %collective-permute-start.5 = (f32[5,32,12,2]{1,3,2,0:T(2,128)S(1)}, f32[5,32,12,2]{1,3,2,0:T(2,128)S(1)}, u32[]{:S(2)}, u32[]{:S(2)}) collective-permute-start(f32[5,32,12,2]{1,3,2,0:T(2,128)S(1)} %copy.327), channel_id=1, source_target_pairs={{16,0},{0,16},{17,1},{1,17},{18,2},{2,18},{19,3},{3,19},{20,4},{4,... | collective-permute-start | bytes 46088 | tf_op jit(solution)/shard_map/ppermute | solution.py:44
  565.5 36.4 %collective-permute-start.6 = (f32[5,32,2,1440]{3,1,2,0:T(8,128)}, f32[5,32,2,1440]{3,1,2,0:T(8,128)}, u32[]{:S(2)}, u32[]{:S(2)}) collective-permute-start(f32[5,32,2,1440]{3,1,2,0:T(8,128)} %get-tuple-element.450), channel_id=1, source_target_pairs={{0,1},{1,2},{2,3},{3,4},{4,5},{5,6},{6,7},{7,8},{8,9},{9,10},{10,1... | collective-permute-start | bytes 5529608 | tf_op jit(solution)/shard_map/ppermute | solution.py:42
  568.1 33.9 %collective-permute-start.7 = (f32[5,32,2,1440]{3,1,2,0:T(8,128)}, f32[5,32,2,1440]{3,1,2,0:T(8,128)}, u32[]{:S(2)}, u32[]{:S(2)}) collective-permute-start(f32[5,32,2,1440]{3,1,2,0:T(8,128)} %get-tuple-element.451), channel_id=1, source_target_pairs={{1,0},{2,1},{3,2},{4,3},{5,4},{6,5},{7,6},{8,7},{9,8},{10,9},{11,1... | collective-permute-start | bytes 5529608 | tf_op jit(solution)/shard_map/ppermute | solution.py:44
  595.4 6.6 slice-start
  595.4 6.6 slice-start.1
  616.6 7.8 copy-start.62
  624.3 6.8 copy-start.52
  631.1 4.8 copy-start.54
  642.8 44.8 %copy-start.60 = (pred[12]{0:T(512)(128)(4,1)S(1)}, pred[12]{0:T(512)(128)(4,1)}, u32[]{:S(2)}) copy-start(pred[12]{0:T(512)(128)(4,1)} %broadcast_compare_fusion) | copy-start | bytes 40
  642.8 44.8 %copy-start.14 = (f32[32,12,1440]{2,0,1:T(8,128)S(1)}, f32[32,12,1440]{2,0,1:T(8,128)}, u32[]{:S(2)}) copy-start(f32[32,12,1440]{2,0,1:T(8,128)} %subtract_sqrt_fusion) | copy-start | bytes 6635524
  712.5 5.2 copy-start.30
  814.8 5.6 copy-start.43
  814.8 5.6 copy-start.46
  814.8 5.7 copy-start.47
  814.8 6.5 copy-start.50
  814.8 14.4 %copy-start.20 = (f32[32,12,1440]{2,0,1:T(8,128)S(1)}, f32[32,12,1440]{2,0,1:T(8,128)}, u32[]{:S(2)}) copy-start(f32[32,12,1440]{2,0,1:T(8,128)} %copy.321) | copy-start | bytes 6635524
  814.8 14.4 %copy-start.56 = (f32[12]{0:T(128)S(1)}, f32[12]{0:T(128)}, u32[]{:S(2)}) copy-start(f32[12]{0:T(128)} %broadcast_multiply_fusion.4) | copy-start | bytes 148
  814.8 14.4 %copy-start.58 = (pred[12]{0:T(512)(128)(4,1)S(1)}, pred[12]{0:T(512)(128)(4,1)}, u32[]{:S(2)}) copy-start(pred[12]{0:T(512)(128)(4,1)} %compare_reduce_fusion) | copy-start | bytes 40
  (35 other events, 118.1 us)
where the time goes:
time: 860 us; the launch traced here: 847 us
  other arithmetic  365 us (42%)
  local copies, waits for them, and re-layouts  360 us (42%)
  blocking collectives  106 us (12%)
  starting transfers between devices  14.5 us (2%)
    add x22, other arithmetic, local_maps(): offset = scale * shifted_by(offset, stride, 0.0) + offset  167 us
    slice x30, local copies, waits for them, and re-layouts, shifted_by(): return jnp.pad(values[..., :-stride], widths, constant_values=fill)  106 us
    mul x10, local copies, waits for them, and re-layouts, local_maps(): offset = scale * shifted_by(offset, stride, 0.0) + offset  89 us
    unnamed x144, local copies, waits for them, and re-layouts  84.8 us
    psum x2, blocking collectives, per_device(): south_total, north_total = lax.psum((south_cap, north_cap), 'lat')  66.2 us
    mul x11, other arithmetic, local_maps(): scale = scale * shifted_by(scale, stride, 1.0)  61.5 us
    concatenate x3, local copies, waits for them, and re-layouts, extended(): jnp.concatenate([lax.ppermute(tail, axis, [(i, (i + 1) % count) for i in...  33.3 us
    add x2, other arithmetic, per_device(): state = state + time_step * rates  29.5 us
  transfers between devices with their start and end apart: 8, of which 0 were waited for; matrix products, arithmetic and copies ran while one was open for 37% of the time, Pallas kernels for 0%

commit v1 on v0

v1 whole, which is shorter than its diff:
```python
import functools

import jax
import jax.numpy as jnp
from jax import lax
from jax.experimental import pallas as pl
from jax.experimental.pallas import tpu as pltpu
from jax.sharding import PartitionSpec as P

SUBSTEPS = 2
LANES = 128
LEVELS = 8

time_step = 0.2
coriolis = 0.5
edge_cosine = 0.5


def angles(index, count):
    return jnp.pi * index.astype(jnp.float32) / count


def lane_scan(scale, offsets, lane, steps):
    for step in range(steps):
        stride = 1 << step
        reached = lane >= stride
        masked = jnp.where(reached, scale, 0.0)
        offsets = [o + masked * pltpu.roll(o, stride, axis=1) for o in offsets]
        scale = jnp.where(reached, scale * pltpu.roll(scale, stride, axis=1), scale)
    return scale, offsets


def rates_kernel(first, band_ref, tab_ref, state_ref, tail_ref, south_ref, north_ref,
                 decay_ref, decay_tail_ref, *refs):
    if first:
        out_ref, prefix_ref, sums_ref, scale_ref, ones_ref, prefix_scale_ref, prefix_ones_ref, prod = refs
    else:
        out_ref, prefix_ref, sums_ref, prod = refs
    rows = state_ref.shape[1]
    cols = state_ref.shape[3]
    main = cols // LANES * LANES
    chunks = main // LANES + 1
    width = chunks * LANES
    lane = lax.broadcasted_iota(jnp.int32, (LEVELS, LANES), 1)
    wide_lane = lax.broadcasted_iota(jnp.int32, (LEVELS, width), 1)
    chunk_steps = max(1, (chunks - 1).bit_length())

    for part in range(4):
        for k in range(2):
            prod[part, k, :, :cols] = south_ref[part, k]
            prod[part, rows + 2 + k, :, :cols] = north_ref[part, k]

    def products(r, carry):
        merid = state_ref[2, r]
        thick = state_ref[0, r]
        prod[0, r + 2, :, :cols] = thick
        prod[1, r + 2, :, :cols] = thick * merid
        prod[2, r + 2, :, :cols] = state_ref[3, r] * merid
        prod[3, r + 2, :, :cols] = state_ref[4, r] * merid
        return carry

    lax.fori_loop(0, rows, products, 0)

    def put(ref, index, value):
        ref[index + (slice(None), slice(0, main))] = value[:, :main]
        ref[index + (slice(None), slice(main, cols))] = value[:, main:cols]

    def row(r, carry):
        def wide(f):
            return jnp.concatenate([state_ref[f, r, :, :main], tail_ref[f, r]], axis=1)

        def slope(q):
            near = pltpu.roll(q, width - 1, axis=1) - pltpu.roll(q, 1, axis=1)
            far = pltpu.roll(q, width - 2, axis=1) - pltpu.roll(q, 2, axis=1)
            return 8.0 * near - far

        lon_factor = tab_ref[r, 5]
        turn = tab_ref[r, 6]
        amount = tab_ref[r, 7]
        thick, zonal, merid = wide(0), wide(1), wide(2)
        heat, tracer = wide(3), wide(4)

        def advect(part, w):
            total = lon_factor * slope(w * zonal)
            for k in range(5):
                total = total + tab_ref[r, k] * prod[part, r + k]
            return total

        lat_slope = 8.0 * (prod[0, r + 3] - prod[0, r + 1]) - (prod[0, r + 4] - prod[0, r])
        rates = [
            advect(1, thick),
            lon_factor * slope(thick) + turn * merid,
            lat_slope * (-1.0 / 12.0) - turn * zonal,
            advect(2, heat),
            advect(3, tracer),
        ]
        rates = [jnp.where(wide_lane < cols, x, 0.0) for x in rates]

        def put_sums(side):
            for f in range(5):
                total = rates[f][:, :LANES]
                for k in range(1, chunks):
                    total = total + rates[f][:, k * LANES:(k + 1) * LANES]
                sums_ref[f, side] = total

        pl.when(r == 0)(lambda: put_sums(0))
        pl.when(r == rows - 1)(lambda: put_sums(1))
        in_band = band_ref[r] > 0
        state = [thick, zonal, merid, heat, tracer]

        @pl.when(jnp.logical_not(in_band))
        def _():
            for f in range(5):
                put(out_ref, (f, r), state[f] + time_step * rates[f])
            if first:
                zero = jnp.zeros((LEVELS, width), jnp.float32)
                put(scale_ref, (r,), zero)
                put(ones_ref, (r,), zero)

        @pl.when(in_band)
        def _():
            count = 6 if first else 5
            whole_scale = jnp.ones((LEVELS, LANES), jnp.float32)
            whole = [jnp.zeros((LEVELS, LANES), jnp.float32) for _ in range(count)]
            for k in range(chunks):
                low, high = k * LANES, (k + 1) * LANES
                last = k == chunks - 1
                decay = decay_tail_ref[r] if last else decay_ref[r, :, low:high]
                gain = jnp.sqrt(1.0 - decay * decay)
                offsets = [gain * x[:, low:high] for x in rates]
                if first:
                    offsets.append(gain)
                scale, offsets = lane_scan(decay, offsets, lane, 7)
                here = lane == k
                to_lane = (k + 1) % LANES
                whole_scale = jnp.where(here, pltpu.roll(scale, to_lane, axis=1), whole_scale)
                whole = [
                    jnp.where(here, pltpu.roll(o, to_lane, axis=1), w)
                    for o, w in zip(offsets, whole)
                ]
                end = cols if last else high
                n = end - low
                for f in range(5):
                    value = state[f][:, low:high] + amount * offsets[f]
                    out_ref[f, r, :, low:end] = value[:, :n]
                if first:
                    scale_ref[r, :, low:end] = scale[:, :n]
                    ones_ref[r, :, low:end] = (time_step - amount * offsets[5])[:, :n]
            whole_scale, whole = lane_scan(whole_scale, whole, lane, chunk_steps)
            start = lane == 0
            before = [jnp.where(start, 0.0, pltpu.roll(w, 1, axis=1)) for w in whole]
            for f in range(5):
                prefix_ref[f, r] = before[f]
            if first:
                prefix_scale_ref[r] = jnp.where(start, 1.0, pltpu.roll(whole_scale, 1, axis=1))
                prefix_ones_ref[r] = before[5]

        return carry

    lax.fori_loop(0, rows, row, 0)


def apply_kernel(state_ref, scale_ref, ones_ref, entry_ref, out_ref):
    rows = state_ref.shape[1]
    cols = state_ref.shape[3]
    main = cols // LANES * LANES
    chunks = main // LANES + 1

    def row(r, carry):
        for f in range(5):
            entry = entry_ref[f, r]
            panel = jnp.broadcast_to(entry[:, LANES - 1:], (LEVELS, LANES))
            for k in range(chunks):
                low = k * LANES
                end = min(low + LANES, cols)
                inflow = jnp.broadcast_to(entry[:, k:k + 1], (LEVELS, LANES))
                out_ref[f, r, :, low:end] = (
                    state_ref[f, r, :, low:end]
                    + scale_ref[r, :, low:end] * inflow[:, :end - low]
                    + ones_ref[r, :, low:end] * panel[:, :end - low]
                )
        return carry

    lax.fori_loop(0, rows, row, 0)


def level_block(shape):
    lead = len(shape) - 2
    return pl.BlockSpec(
        tuple(shape[:-2]) + (LEVELS, shape[-1]), lambda g: (0,) * lead + (g, 0)
    )


def shaped(shape):
    return jax.ShapeDtypeStruct(shape, jnp.float32)


def call_rates(first, band, table, state, tail, south, north, decay, decay_tail):
    fields, rows, levels, cols = state.shape
    width = cols // LANES * LANES + LANES
    outs = [
        shaped(state.shape),
        shaped((fields, rows, levels, LANES)),
        shaped((fields, 2, levels, LANES)),
    ]
    if first:
        outs += [shaped((rows, levels, cols))] * 2 + [shaped((rows, levels, LANES))] * 2
    arrays = (state, tail, south, north, decay, decay_tail)
    smem = pl.BlockSpec(memory_space=pltpu.SMEM)
    return pl.pallas_call(
        functools.partial(rates_kernel, first),
        grid=(levels // LEVELS,),
        in_specs=[smem, smem] + [level_block(x.shape) for x in arrays],
        out_specs=[level_block(x.shape) for x in outs],
        out_shape=outs,
        scratch_shapes=[pltpu.VMEM((4, rows + 4, LEVELS, width), jnp.float32)],
        compiler_params=pltpu.CompilerParams(vmem_limit_bytes=48 * 1024 * 1024),
    )(band, table, *arrays)


def call_apply(state, scale, ones, entry):
    levels = state.shape[2]
    arrays = (state, scale, ones, entry)
    return pl.pallas_call(
        apply_kernel,
        grid=(levels // LEVELS,),
        in_specs=[level_block(x.shape) for x in arrays],
        out_specs=level_block(state.shape),
        out_shape=shaped(state.shape),
        compiler_params=pltpu.CompilerParams(vmem_limit_bytes=48 * 1024 * 1024),
    )(*arrays)


def shift(x, axis, step, closed):
    count = lax.axis_size(axis)
    if closed:
        pairs = [(i, (i + step) % count) for i in range(count)]
    else:
        pairs = [(i, i + step) for i in range(count) if 0 <= i + step < count]
    return lax.ppermute(x, axis, pairs)


def lon_halos(state):
    cols = state.shape[3]
    head = jnp.moveaxis(state[..., :2], 3, 0)
    tail = jnp.moveaxis(state[..., cols - 2:], 3, 0)
    if lax.axis_size("lon") == 2:
        both = shift(jnp.concatenate([head, tail]), "lon", 1, True)
        west, east = both[2:], both[:2]
    else:
        west = shift(tail, "lon", 1, True)
        east = shift(head, "lon", -1, True)
    return jnp.moveaxis(west, 0, 3), jnp.moveaxis(east, 0, 3)


def lat_halos(state):
    rows = state.shape[1]

    def parts(strip):
        return jnp.stack(
            [strip[0], strip[0] * strip[2], strip[3] * strip[2], strip[4] * strip[2]]
        )

    south = shift(parts(state[:, rows - 2:]), "lat", 1, False)
    north = shift(parts(state[:, :2]), "lat", -1, False)
    return south, north


def over_lon(x):
    if lax.axis_size("lon") == 2:
        other = shift(x, "lon", 1, True)
        mine = lax.axis_index("lon") == 0
        return [jnp.where(mine, x, other), jnp.where(mine, other, x)]
    everything = lax.all_gather(x, "lon")
    return [everything[k] for k in range(lax.axis_size("lon"))]


def per_device(state, decay, band_rows):
    state = jnp.transpose(state, (0, 2, 1, 3))
    decay = jnp.transpose(decay, (1, 0, 2))
    fields, local_rows, levels, cols = state.shape
    lat_count, lon_count = lax.axis_size("lat"), lax.axis_size("lon")
    total_rows = local_rows * lat_count
    total_cols = cols * lon_count
    main = cols // LANES * LANES
    chunks = main // LANES + 1
    spare = main + LANES - cols - 4
    lat_index, lon_index = lax.axis_index("lat"), lax.axis_index("lon")
    rows = lat_index * local_rows + jnp.arange(local_rows, dtype=jnp.int32)
    centre = angles(2 * rows + 1, 2 * total_rows)
    cosine = jnp.sin(centre)
    sine = -jnp.cos(centre)
    face_rows = lat_index * local_rows + jnp.arange(local_rows + 1, dtype=jnp.int32)
    face_cos = jnp.sin(angles(face_rows, total_rows))
    low, high = face_cos[:-1], face_cos[1:]
    over = -1.0 / (12.0 * cosine)
    amount = time_step * cosine / edge_cosine
    table = jnp.stack(
        [
            low * over,
            (-high - 7.0 * low) * over,
            7.0 * (high - low) * over,
            (7.0 * high + low) * over,
            -high * over,
            over,
            coriolis * sine,
            amount,
        ],
        axis=1,
    )
    in_band = jnp.any(rows[:, None] == band_rows[None, :], axis=1)
    band = in_band.astype(jnp.int32)
    southern = rows < total_rows // 2
    ends = jnp.stack([lat_index == 0, lat_index == lat_count - 1])
    decay_tail = jnp.pad(
        decay[:, :, main:], ((0, 0), (0, 0), (0, main + LANES - cols)), constant_values=1.0
    )
    lanes = jnp.arange(LANES)
    gap = jnp.zeros((fields, local_rows, levels, spare), jnp.float32)
    for substep in range(SUBSTEPS):
        south, north = lat_halos(state)
        west, east = lon_halos(state)
        tail = jnp.concatenate([state[..., main:], east, gap, west], axis=3)
        outs = call_rates(
            substep == 0, band, table, state, tail, south, north, decay, decay_tail
        )
        if substep == 0:
            partial, prefix, sums, scale, ones, prefix_scale, prefix_ones = outs
        else:
            partial, prefix, sums = outs
        caps = jnp.where(ends[None, :, None], jnp.sum(sums, axis=-1), 0.0)
        caps = lax.psum(caps, ("lon", "lat")) / total_cols
        maps = jnp.concatenate(
            [
                prefix[..., chunks],
                prefix_scale[None, ..., chunks],
                prefix_ones[None, ..., chunks],
            ]
        )
        maps = over_lon(maps)
        panel = jnp.where(southern[None, :, None], caps[:, None, 0], caps[:, None, 1])
        pre_scale, pre_offset = jnp.ones_like(maps[0][:1]), jnp.zeros_like(panel)
        all_scale, all_offset = pre_scale, pre_offset
        for k in range(lon_count):
            step_scale = maps[k][5:6]
            step_offset = maps[k][:5] - panel * maps[k][6:]
            all_offset = step_scale * all_offset + step_offset
            all_scale = step_scale * all_scale
            reached = k < lon_index
            pre_scale = jnp.where(reached, all_scale, pre_scale)
            pre_offset = jnp.where(reached, all_offset, pre_offset)
        inflow = pre_scale * (all_offset / (1.0 - all_scale)) + pre_offset
        entry = amount[:, None, None] * (
            prefix
            + prefix_scale[None] * inflow[..., None]
            - panel[..., None] * prefix_ones[None]
        )
        entry = jnp.where(lanes == LANES - 1, panel[..., None], entry)
        entry = jnp.where(in_band[:, None, None], entry, 0.0)
        state = call_apply(partial, scale, ones, entry)
    return jnp.transpose(state, (0, 2, 1, 3))


def solution(mesh):
    placed = (P(None, None, "lat", "lon"), P(None, "lat", "lon"), P())
    return jax.shard_map(
        per_device,
        mesh=mesh,
        in_specs=placed,
        out_specs=P(None, None, "lat", "lon"),
        check_vma=False,
    )
```

time: 860 us -> 368 us (0.43); the launches traced: 847 us -> 366 us
  local copies, waits for them, and re-layouts: 360 us -> 21.2 us
  other arithmetic: 365 us -> 26.3 us
  Pallas kernels: 0 us -> 177 us
  blocking collectives: 106 us -> 116 us
    add x28 -> x0, other arithmetic: 197 us -> none  [the longest x22 167 us: local_maps(): offset = scale * shifted_by(offset, stride, 0.0) + offset]
    pallas_call x0 -> x4, Pallas kernels: none -> 177 us  [the longest x2 151 us: call_rates(): pl.pallas_call(functools.partial(rates_kernel, first), grid=(levels // LE...]
    mul x21 -> x3, other arithmetic: 117 us -> 0.08 us  [the longest x1 0.06 us: per_device(): coriolis * sine]
    slice x41 -> x12, local copies, waits for them, and re-layouts: 120 us -> 4.61 us  [the longest x3 1.27 us: per_device(): tail = jnp.concatenate([state[..., main:], east, gap, west], axis=3)]
    mul x12 -> x0, local copies, waits for them, and re-layouts: 98.9 us -> none  [the longest x10 89 us: local_maps(): offset = scale * shifted_by(offset, stride, 0.0) + offset]
    unnamed x144 -> x38, local copies, waits for them, and re-layouts: 84.8 us -> 8.61 us
    concatenate x3 -> x1, local copies, waits for them, and re-layouts: 33.3 us -> 0.07 us  [per_device(): tail = jnp.concatenate([state[..., main:], east, gap, west], axis=3)]
    psum x6 -> x2, blocking collectives: 92.4 us -> 116 us  [per_device(): caps = lax.psum(caps, ('lon', 'lat')) / total_cols]
  transfers between devices with their start and end apart: 8 -> 8, of which waited for: 0 -> 3; matrix products, arithmetic and copies ran while one was open for 37% -> 8% of each run, Pallas kernels for 0% -> 0%
where the time goes in v1:
time: 368 us; the launch traced here: 366 us
  Pallas kernels  177 us (48%)
  blocking collectives  116 us (32%)
  other arithmetic  26.3 us (7%)
  local copies, waits for them, and re-layouts  21.2 us (6%)
  starting transfers between devices  17.9 us (5%)
  waiting for transfers between devices  7.29 us (2%)
    pallas_call x2, Pallas kernels, call_rates(): pl.pallas_call(functools.partial(rates_kernel, first), grid=(levels // LE...  151 us
    psum x2, blocking collectives, per_device(): caps = lax.psum(caps, ('lon', 'lat')) / total_cols  116 us
    pallas_call x2, Pallas kernels, call_apply(): pl.pallas_call(apply_kernel, grid=(levels // LEVELS,), in_specs=[level_bl...  26.7 us
    ppermute x8, starting transfers between devices, shift(): return lax.ppermute(x, axis, pairs)  17.9 us
    unnamed x38, local copies, waits for them, and re-layouts  8.61 us
  transfers between devices with their start and end apart: 8, of which 3 were waited for; matrix products, arithmetic and copies ran while one was open for 8% of the time, Pallas kernels for 0%

profile of v1, /device:TPU:0, one launch (start us, length us, event | category | flops | bytes accessed | tf_op | source)
XLA Modules:
  0.0 366.4 jit_solution(59554837631542795)
XLA Ops:
  0.0 1.9 slice_bitcast_fusion.3
  2.8 3.0 collective-permute-start
  5.9 2.1 fusion.7
  8.0 1.3 pad_maximum_fusion
  9.3 2.6 collective-permute-start.1
  11.9 1.3 pad_maximum_fusion.1
  13.2 1.3 collective-permute-start.2
  16.0 0.7 pad_add_fusion
  16.7 1.3 slice.230
  18.4 0.9 slice.243
  20.1 1.4 copy.83
  21.5 1.9 pad_maximum_fusion.4.tail_ref
  23.4 80.1 %shard_map.37 = (f32[5,12,32,1440]{3,2,1,0:T(8,128)}, f32[5,12,32,128]{3,2,1,0:T(8,128)S(1)}, f32[5,2,32,128]{3,2,1,0:T(8,128)S(1)}, f32[12,32,1440]{2,1,0:T(8,1...) custom-call(s32[12]{0:T(128)S(1)} %convert_element_type.30.band_ref, ...), custom_call_target="tpu_custom_call" | custom-call | tf_op jit(solution)/shard_map/pallas_call | solution.py:210
  103.7 62.7 %psum.14 = f32[5,2,32]{2,1,0:T(2,128)S(1)} all-reduce(f32[5,2,32]{2,1,0:T(2,128)S(1)} %broadcast_select_fusion.7), channel_id=1, replica_groups=mesh['lon'=2,'lat'=16] {'lon','lat'}, use_global_device_ids=true, to_apply=%region_2.3 | all-reduce | flops 320 | bytes 2560 | tf_op jit(solution)/shard_map/psum | solution.py:332
  167.6 2.3 collective-permute-start.3
  169.9 2.1 collective-permute-done.3
  172.1 0.7 broadcast_select_fusion.5
  172.8 1.7 select_select_fusion.1.entry_ref
  174.6 1.7 copy-done.1
  176.2 13.4 %shard_map.38.state_ref = f32[5,12,32,1440]{3,2,1,0:T(8,128)} custom-call(f32[5,12,32,1440]{3,2,1,0:T(8,128)} %get-tuple-element.15.state_ref, f32[12,32,1440]{2,1,0:T(8,128)S(1)} %copy-done, f32[12,32,1440]{2,1,0:T(8,128)S(1)} %copy-done.1, f32[5,12,32,128]{3,2,1,0:T(8,128)S(1)} %select_select_fusion.1.entry_ref), custom_call_target="tpu_custom_call" | custom-call | tf_op jit(solution)/shard_map/pallas_call | solution.py:224
  189.6 2.3 fusion.6
  191.9 1.3 pad_maximum_fusion.2
  193.1 2.7 collective-permute-start.5
  195.8 1.3 pad_maximum_fusion.3
  197.2 1.3 collective-permute-start.6
  198.5 1.3 slice_bitcast_fusion.1
  199.8 2.2 copy.72
  202.0 1.0 copy.73
  203.1 0.9 pad_maximum_fusion.7
  204.0 2.1 collective-permute-start.4
  206.1 3.0 collective-permute-done.4
  209.1 0.7 fusion.8
  209.8 2.2 copy.84
  212.0 2.2 copy.85
  214.2 2.1 pad_maximum_fusion.5.tail_ref
  216.3 70.6 %shard_map.39 = (f32[5,12,32,1440]{3,2,1,0:T(8,128)}, f32[5,12,32,128]{3,2,1,0:T(8,128)S(1)}, f32[5,2,32,128]{3,2,1,0:T(8,128)S(1)}) custom-call(s32[12]{0:T(128)S(1)} %convert_element_type.30.band_ref, f32[12,8]{1,0:T(8,128)S(1)} %stack.59.tab_ref, f32[5,12,32,1440]{3,2,1,0:T(8,128)} %shard_map.38.state_ref, ...), custom_call_target="tpu_custom_call" | custom-call | tf_op jit(solution)/shard_map/pallas_call | solution.py:210
  286.9 0.7 copy-done.7
  287.6 1.7 reduce_sum.19
  289.2 0.8 broadcast_select_fusion.6
  290.0 53.2 %psum.15 = f32[5,2,32]{2,1,0:T(2,128)} all-reduce(f32[5,2,32]{2,1,0:T(2,128)S(1)} %broadcast_select_fusion.6), channel_id=1, replica_groups=mesh['lon'=2,'lat'=16] {'lon','lat'}, use_global_device_ids=true, to_apply=%region_4.5 | all-reduce | flops 320 | bytes 2560 | tf_op jit(solution)/shard_map/psum | solution.py:332
  343.3 0.7 broadcast_multiply_fusion
  344.6 0.9 pad_maximum_fusion.8
  345.5 2.6 collective-permute-start.7
  348.1 2.1 collective-permute-done.7
  350.2 0.7 broadcast_select_fusion
  351.0 0.7 broadcast_select_fusion.4
  351.7 1.4 select_select_fusion.entry_ref
  353.1 13.3 %shard_map.40 = f32[5,12,32,1440]{3,2,1,0:T(8,128)} custom-call(f32[5,12,32,1440]{3,2,1,0:T(8,128)} %get-tuple-element.22.state_ref, f32[12,32,1440]{2,1,0:T(8,128)S(1)} %copy-done, f32[12,32,1440]{2,1,0:T(8,128)S(1)} %copy-done.2, f32[5,12,32,128]{3,2,1,0:T(8,128)S(1)} %select_select_fusion.entry_ref), custom_call_target="tpu_custom_call" | custom-call | tf_op jit(solution)/shard_map/pallas_call | solution.py:224
  (76 shorter events, 5.6 us)
Async XLA Ops:
  2.8 16.7 %collective-permute-start = (f32[4,5,12,32]{3,0,2,1:T(4,128)S(1)}, f32[4,5,12,32]{3,0,2,1:T(4,128)S(1)}, u32[]{:S(2)}, u32[]{:S(2)}) collective-permute-start(f32[4,5,12,32]{3,0,2,1:T(4,128)S(1)} %pad_maximum_fusion.6), channel_id=1, source_target_pairs={{0,16},{16,0},{1,17},{17,1},{2,18},{18,2},{3,19},{19,3},{4,20},{20... | collective-permute-start | bytes 92168 | tf_op jit(solution)/shard_map/ppermute | solution.py:240
  9.3 14.1 %collective-permute-start.1 = (f32[4,2,32,1440]{3,2,1,0:T(8,128)}, f32[4,2,32,1440]{3,2,1,0:T(8,128)}, u32[]{:S(2)}, u32[]{:S(2)}) collective-permute-start(f32[4,2,32,1440]{3,2,1,0:T(8,128)} %pad_maximum_fusion), channel_id=1, source_target_pairs={{0,1},{1,2},{2,3},{3,4},{4,5},{5,6},{6,7},{7,8},{8,9},{9,10},{10,1... | collective-permute-start | bytes 4423688 | tf_op jit(solution)/shard_map/ppermute | solution.py:240
  11.9 3.9 %copy-start.14 = (s32[64]{0:T(128)S(1)}, s32[64]{0:T(128)}, u32[]{:S(2)}) copy-start(s32[64]{0:T(128)} %param.5) | copy-start | bytes 772
  13.2 10.2 %collective-permute-start.2 = (f32[4,2,32,1440]{3,2,1,0:T(8,128)}, f32[4,2,32,1440]{3,2,1,0:T(8,128)}, u32[]{:S(2)}, u32[]{:S(2)}) collective-permute-start(f32[4,2,32,1440]{3,2,1,0:T(8,128)} %pad_maximum_fusion.1), channel_id=1, source_target_pairs={{1,0},{2,1},{3,2},{4,3},{5,4},{6,5},{7,6},{8,7},{9,8},{10,9},{11,1... | collective-permute-start | bytes 4423688 | tf_op jit(solution)/shard_map/ppermute | solution.py:240
  16.0 2.5 copy-start.11
  19.5 3.9 %copy-start.12 = (f32[128]{0:T(128)}, f32[128]{0:T(128)S(1)}, u32[]{:S(2)}) copy-start(f32[128]{0:T(128)S(1)} %pad.37.clone) | copy-start | bytes 1540
  23.4 80.3 %copy-start.13 = (pred[2]{0:T(512)(128)(4,1)S(1)}, pred[2]{0:T(512)(128)(4,1)}, u32[]{:S(2)}) copy-start(pred[2]{0:T(512)(128)(4,1)} %pad_add_fusion) | copy-start | bytes 10
  103.5 64.0 %copy-start.3 = (f32[12,32,128]{2,1,0:T(8,128)}, f32[12,32,128]{2,1,0:T(8,128)S(1)}, u32[]{:S(2)}) copy-start(f32[12,32,128]{2,1,0:T(8,128)S(1)} %get-tuple-element.20) | copy-start | bytes 589828
  103.5 64.0 %copy-start.5 = (f32[12,32,128]{2,1,0:T(8,128)}, f32[12,32,128]{2,1,0:T(8,128)S(1)}, u32[]{:S(2)}) copy-start(f32[12,32,128]{2,1,0:T(8,128)S(1)} %get-tuple-element.21) | copy-start | bytes 589828
  166.7 7.9 %copy-start.9 = (f32[12,32]{1,0:T(8,128)}, f32[12,32]{1,0:T(8,128)S(1)}, u32[]{:S(2)}) copy-start(f32[12,32]{1,0:T(8,128)S(1)} %slice_reduce_fusion.3) | copy-start | bytes 4612
  166.9 7.6 %copy-start.10 = (f32[12,32]{1,0:T(8,128)}, f32[12,32]{1,0:T(8,128)S(1)}, u32[]{:S(2)}) copy-start(f32[12,32]{1,0:T(8,128)S(1)} %slice_reduce_fusion.2) | copy-start | bytes 4612
  167.5 7.0 %copy-start = (f32[12,32,1440]{2,1,0:T(8,128)S(1)}, f32[12,32,1440]{2,1,0:T(8,128)}, u32[]{:S(2)}) copy-start(f32[12,32,1440]{2,1,0:T(8,128)} %get-tuple-element.16.scale_ref) | copy-start | bytes 6635524
  167.6 4.5 %collective-permute-start.3 = (f32[7,12,32]{2,1,0:T(8,128)S(1)}, f32[7,12,32]{2,1,0:T(8,128)S(1)}, u32[]{:S(2)}, u32[]{:S(2)}) collective-permute-start(f32[7,12,32]{2,1,0:T(8,128)S(1)} %pad_maximum_fusion.9), channel_id=1, source_target_pairs={{0,16},{16,0},{1,17},{17,1},{2,18},{18,2},{3,19},{19,3},{4,20},{20... | collective-permute-start | bytes 32264 | tf_op jit(solution)/shard_map/ppermute | solution.py:240
  174.5 1.7 copy-start.1
  189.6 8.9 %copy-start.8 = (f32[5,12,32,1440]{3,2,1,0:T(8,128)S(1)}, f32[5,12,32,1440]{3,2,1,0:T(8,128)}, u32[]{:S(2)}) copy-start(f32[5,12,32,1440]{3,2,1,0:T(8,128)} %shard_map.38.state_ref) | copy-start | bytes 33177604
  193.1 23.2 %collective-permute-start.5 = (f32[4,2,32,1440]{3,2,1,0:T(8,128)}, f32[4,2,32,1440]{3,2,1,0:T(8,128)}, u32[]{:S(2)}, u32[]{:S(2)}) collective-permute-start(f32[4,2,32,1440]{3,2,1,0:T(8,128)} %pad_maximum_fusion.2), channel_id=1, source_target_pairs={{0,1},{1,2},{2,3},{3,4},{4,5},{5,6},{6,7},{7,8},{8,9},{9,10},{10,1... | collective-permute-start | bytes 4423688 | tf_op jit(solution)/shard_map/ppermute | solution.py:240
  197.2 19.2 %collective-permute-start.6 = (f32[4,2,32,1440]{3,2,1,0:T(8,128)}, f32[4,2,32,1440]{3,2,1,0:T(8,128)}, u32[]{:S(2)}, u32[]{:S(2)}) collective-permute-start(f32[4,2,32,1440]{3,2,1,0:T(8,128)} %pad_maximum_fusion.3), channel_id=1, source_target_pairs={{1,0},{2,1},{3,2},{4,3},{5,4},{6,5},{7,6},{8,7},{9,8},{10,9},{11,1... | collective-permute-start | bytes 4423688 | tf_op jit(solution)/shard_map/ppermute | solution.py:240
  204.0 5.1 %collective-permute-start.4 = (f32[4,5,12,32]{3,0,2,1:T(4,128)S(1)}, f32[4,5,12,32]{3,0,2,1:T(4,128)S(1)}, u32[]{:S(2)}, u32[]{:S(2)}) collective-permute-start(f32[4,5,12,32]{3,0,2,1:T(4,128)S(1)} %pad_maximum_fusion.7), channel_id=1, source_target_pairs={{0,16},{16,0},{1,17},{17,1},{2,18},{18,2},{3,19},{19,3},{4,20},{20... | collective-permute-start | bytes 92168 | tf_op jit(solution)/shard_map/ppermute | solution.py:240
  206.1 8.1 %slice-start = ((f32[5,12,32,1440]{3,2,1,0:T(8,128)}), f32[5,12,32,32]{3,2,1,0:T(8,128)S(1)}, s32[]{:S(2)}) async-start(f32[5,12,32,1440]{3,2,1,0:T(8,128)} %shard_map.38.state_ref), calls=%async_computation | async-start | bytes 1966080 | tf_op jit(solution)/shard_map/slice | solution.py:323
  286.9 0.7 copy-start.7
  287.6 64.1 %copy-start.4 = (f32[12,32,128]{2,1,0:T(8,128)S(1)}, f32[12,32,128]{2,1,0:T(8,128)}, u32[]{:S(2)}) copy-start(f32[12,32,128]{2,1,0:T(8,128)} %copy-done.3) | copy-start | bytes 589828
  343.3 8.4 %copy-start.6 = (f32[12,32,128]{2,1,0:T(8,128)S(1)}, f32[12,32,128]{2,1,0:T(8,128)}, u32[]{:S(2)}) copy-start(f32[12,32,128]{2,1,0:T(8,128)} %copy-done.5) | copy-start | bytes 589828
  344.6 8.5 %copy-start.2 = (f32[12,32,1440]{2,1,0:T(8,128)S(1)}, f32[12,32,1440]{2,1,0:T(8,128)}, u32[]{:S(2)}) copy-start(f32[12,32,1440]{2,1,0:T(8,128)} %get-tuple-element.17.ones_ref) | copy-start | bytes 6635524
  345.5 4.8 %collective-permute-start.7 = (f32[7,12,32]{2,1,0:T(8,128)S(1)}, f32[7,12,32]{2,1,0:T(8,128)S(1)}, u32[]{:S(2)}, u32[]{:S(2)}) collective-permute-start(f32[7,12,32]{2,1,0:T(8,128)S(1)} %pad_maximum_fusion.8), channel_id=1, source_target_pairs={{0,16},{16,0},{1,17},{17,1},{2,18},{18,2},{3,19},{19,3},{4,20},{20... | collective-permute-start | bytes 32264 | tf_op jit(solution)/shard_map/ppermute | solution.py:240

commit v2 on v1

--- a/solution.py
+++ b/solution.py
@@ -184,6 +184,70 @@
     lax.fori_loop(0, rows, row, 0)
 
 
+def caps_kernel(caps_ref, out_ref, send_sem, recv_sem):
+    mine, count = lax.axis_index("lat"), lax.axis_size("lat")
+    barrier = pltpu.get_barrier_semaphore()
+    poles = (0, count - 1)
+
+    def greet(pole):
+        pl.semaphore_signal(
+            barrier, inc=1, device_id={"lat": pole}, device_id_type=pl.DeviceIdType.MESH
+        )
+
+    def copy(side, other):
+        return pltpu.make_async_remote_copy(
+            src_ref=caps_ref.at[side],
+            dst_ref=out_ref.at[side],
+            send_sem=send_sem.at[other],
+            recv_sem=recv_sem.at[side],
+            device_id={"lat": other},
+            device_id_type=pl.DeviceIdType.MESH,
+        )
+
+    for side, pole in enumerate(poles):
+        pl.when(mine != pole)(functools.partial(greet, pole))
+    for side, pole in enumerate(poles):
+
+        @pl.when(mine == pole)
+        def _():
+            pl.semaphore_wait(barrier, count - 1)
+            out_ref[side] = caps_ref[side]
+
+            def start(step, carry):
+                copy(side, lax.rem(pole + step, count)).start()
+                return carry
+
+            lax.fori_loop(1, count, start, 0)
+
+    for side, pole in enumerate(poles):
+
+        @pl.when(mine != pole)
+        def _():
+            copy(side, pole).wait_recv()
+
+        @pl.when(mine == pole)
+        def _():
+            def finish(step, carry):
+                copy(side, lax.rem(pole + step, count)).wait_send()
+                return carry
+
+            lax.fori_loop(1, count, finish, 0)
+
+
+def share_caps(caps):
+    return pl.pallas_call(
+        caps_kernel,
+        out_shape=shaped(caps.shape),
+        in_specs=[pl.BlockSpec(memory_space=pltpu.VMEM)],
+        out_specs=pl.BlockSpec(memory_space=pltpu.VMEM),
+        scratch_shapes=[
+            pltpu.SemaphoreType.DMA((lax.axis_size("lat"),)),
+            pltpu.SemaphoreType.DMA((2,)),
+        ],
+        compiler_params=pltpu.CompilerParams(collective_id=0, has_side_effects=True),
+    )(caps)
+
+
 def level_block(shape):
     lead = len(shape) - 2
     return pl.BlockSpec(
@@ -311,7 +375,6 @@
     in_band = jnp.any(rows[:, None] == band_rows[None, :], axis=1)
     band = in_band.astype(jnp.int32)
     southern = rows < total_rows // 2
-    ends = jnp.stack([lat_index == 0, lat_index == lat_count - 1])
     decay_tail = jnp.pad(
         decay[:, :, main:], ((0, 0), (0, 0), (0, main + LANES - cols)), constant_values=1.0
     )
@@ -328,22 +391,22 @@
             partial, prefix, sums, scale, ones, prefix_scale, prefix_ones = outs
         else:
             partial, prefix, sums = outs
-        caps = jnp.where(ends[None, :, None], jnp.sum(sums, axis=-1), 0.0)
-        caps = lax.psum(caps, ("lon", "lat")) / total_cols
+        caps = share_caps(jnp.moveaxis(jnp.sum(sums, axis=-1), 1, 0))
         maps = jnp.concatenate(
             [
                 prefix[..., chunks],
                 prefix_scale[None, ..., chunks],
                 prefix_ones[None, ..., chunks],
+                jnp.where(southern[None, :, None], caps[0][:, None], caps[1][:, None]),
             ]
         )
         maps = over_lon(maps)
-        panel = jnp.where(southern[None, :, None], caps[:, None, 0], caps[:, None, 1])
+        panel = sum(x[7:] for x in maps) / total_cols
         pre_scale, pre_offset = jnp.ones_like(maps[0][:1]), jnp.zeros_like(panel)
         all_scale, all_offset = pre_scale, pre_offset
         for k in range(lon_count):
             step_scale = maps[k][5:6]
-            step_offset = maps[k][:5] - panel * maps[k][6:]
+            step_offset = maps[k][:5] - panel * maps[k][6:7]
             all_offset = step_scale * all_offset + step_offset
             all_scale = step_scale * all_scale
             reached = k < lon_index

time: 368 us -> 310 us (0.84)
  blocking collectives: 116 us -> 0 us
  Pallas kernels: 177 us -> 230 us
  waiting for transfers between devices: 7.29 us -> 13.9 us
  starting transfers between devices: 17.9 us -> 11.5 us
  local copies, waits for them, and re-layouts: 21.2 us -> 27.5 us
    psum x2 -> x0, blocking collectives: 116 us -> none  [per_device(): caps = lax.psum(caps, ('lon', 'lat')) / total_cols]
    pallas_call x0 -> x2, Pallas kernels: none -> 53.4 us  [share_caps(): pl.pallas_call(caps_kernel, out_shape=shaped(caps.shape), in_specs=[pl.Bl...]
    ppermute x8, waiting for transfers between devices: 7.29 us -> 13.9 us  [shift(): return lax.ppermute(x, axis, pairs)]
    ppermute x8, starting transfers between devices: 17.9 us -> 11.5 us  [shift(): return lax.ppermute(x, axis, pairs)]
    unnamed x38 -> x42, local copies, waits for them, and re-layouts: 8.61 us -> 12.2 us
  transfers between devices with their start and end apart: 8 -> 8, of which waited for: 3 -> 3; matrix products, arithmetic and copies ran while one was open for 8% -> 9% of each run, Pallas kernels for 0% -> 0%
where the time goes in v2:
time: 310 us; the launch traced here: 309 us
  Pallas kernels  230 us (74%)
  local copies, waits for them, and re-layouts  27.5 us (9%)
  other arithmetic  25.1 us (8%)
  waiting for transfers between devices  13.9 us (4%)
  starting transfers between devices  11.5 us (4%)
    pallas_call x2, Pallas kernels, call_rates(): pl.pallas_call(functools.partial(rates_kernel, first), grid=(levels // LE...  150 us
    pallas_call x2, Pallas kernels, share_caps(): pl.pallas_call(caps_kernel, out_shape=shaped(caps.shape), in_specs=[pl.Bl...  53.4 us
    pallas_call x2, Pallas kernels, call_apply(): pl.pallas_call(apply_kernel, grid=(levels // LEVELS,), in_specs=[level_bl...  26.6 us
    ppermute x8, waiting for transfers between devices, shift(): return lax.ppermute(x, axis, pairs)  13.9 us
    unnamed x42, local copies, waits for them, and re-layouts  12.2 us
    ppermute x8, starting transfers between devices, shift(): return lax.ppermute(x, axis, pairs)  11.5 us
  transfers between devices with their start and end apart: 8, of which 3 were waited for; matrix products, arithmetic and copies ran while one was open for 9% of the time, Pallas kernels for 0%

profile of v2, /device:TPU:0, one launch (start us, length us, event | category | flops | bytes accessed | tf_op | source)
XLA Modules:
  0.0 308.8 jit_solution(497904553084066203)
XLA Ops:
  0.0 1.9 slice_bitcast_fusion.3
  2.8 3.0 collective-permute-start
  5.9 2.1 fusion.13
  8.0 1.3 pad_maximum_fusion
  9.2 1.5 collective-permute-start.1
  10.8 1.3 pad_maximum_fusion.1
  12.1 1.3 collective-permute-start.2
  15.1 1.3 slice.246
  16.9 0.9 slice.259
  18.1 1.4 copy.84
  19.5 1.4 copy.85
  20.9 2.1 pad_maximum_fusion.4.tail_ref
  23.0 1.1 copy-done.7
  24.1 1.4 copy-done.8
  25.5 80.0 %shard_map.37 = (f32[5,12,32,1440]{3,2,1,0:T(8,128)}, f32[5,12,32,128]{3,2,1,0:T(8,128)S(1)}, f32[5,2,32,128]{3,2,1,0:T(8,128)S(1)}, f32[12,32,1440]{2,1,0:T(8,1...) custom-call(s32[12]{0:T(128)S(1)} %convert_element_type.30.band_ref, ...), custom_call_target="tpu_custom_call" | custom-call | tf_op jit(solution)/shard_map/pallas_call | solution.py:274
  106.3 32.3 %shard_map.38 = f32[2,5,32]{2,1,0:T(8,128)} custom-call(f32[2,5,32]{2,1,0:T(8,128)} %bitcast.84), custom_call_target="tpu_custom_call" | custom-call | tf_op jit(solution)/shard_map/pallas_call | solution.py:238
  138.5 0.7 slice_bitcast_fusion.9
  140.4 0.7 fusion
  142.2 4.0 %collective-permute-done.3 = f32[12,12,32]{2,1,0:T(8,128)} collective-permute-done((f32[12,12,32]{2,1,0:T(8,128)}, f32[12,12,32]{2,1,0:T(8,128)}, u32[]{:S(2)}, u32[]{:S(2)}) %collective-permute-start.3) | collective-permute-done | bytes 18464 | tf_op jit(solution)/shard_map/ppermute | solution.py:304
  146.2 0.9 broadcast_select_fusion.3
  147.2 1.7 select_select_fusion.1.entry_ref
  148.9 1.7 copy-done.1
  150.6 13.3 %shard_map.39.state_ref = f32[5,12,32,1440]{3,2,1,0:T(8,128)} custom-call(f32[5,12,32,1440]{3,2,1,0:T(8,128)} %get-tuple-element.15.state_ref, f32[12,32,1440]{2,1,0:T(8,128)S(1)} %copy-done, f32[12,32,1440]{2,1,0:T(8,128)S(1)} %copy-done.1, f32[5,12,32,128]{3,2,1,0:T(8,128)S(1)} %select_select_fusion.1.entry_ref), custom_call_target="tpu_custom_call" | custom-call | tf_op jit(solution)/shard_map/pallas_call | solution.py:288
  163.9 2.3 fusion.12
  166.1 1.3 pad_maximum_fusion.2
  167.4 2.7 collective-permute-start.5
  170.1 1.3 pad_maximum_fusion.3
  171.4 1.3 collective-permute-start.6
  172.7 1.3 slice_bitcast_fusion.1
  174.1 2.2 copy.77
  176.3 1.0 copy.78
  177.4 0.9 pad_maximum_fusion.11
  178.9 5.5 %collective-permute-done.4 = f32[4,5,12,32]{3,0,2,1:T(4,128)S(1)} collective-permute-done((f32[4,5,12,32]{3,0,2,1:T(4,128)S(1)}, f32[4,5,12,32]{3,0,2,1:T(4,128)S(1)}, u32[]{:S(2)}, u32[]{:S(2)}) %collective-permute-start.4) | collective-permute-done | bytes 30752 | tf_op jit(solution)/shard_map/ppermute | solution.py:304
  184.4 0.7 fusion.14
  185.1 2.2 copy.86
  187.3 2.2 copy.87
  189.6 2.1 pad_maximum_fusion.5.tail_ref
  191.7 70.3 %shard_map.40 = (f32[5,12,32,1440]{3,2,1,0:T(8,128)}, f32[5,12,32,128]{3,2,1,0:T(8,128)S(1)}, f32[5,2,32,128]{3,2,1,0:T(8,128)S(1)}) custom-call(s32[12]{0:T(128)S(1)} %convert_element_type.30.band_ref, f32[12,8]{1,0:T(8,128)S(1)} %stack.50.tab_ref, f32[5,12,32,1440]{3,2,1,0:T(8,128)} %shard_map.39.state_ref, ...), custom_call_target="tpu_custom_call" | custom-call | tf_op jit(solution)/shard_map/pallas_call | solution.py:274
  262.0 0.7 copy-done.9
  262.7 1.1 reduce_sum.19
  264.4 21.2 %shard_map.41 = f32[2,5,32]{2,1,0:T(8,128)} custom-call(f32[2,5,32]{2,1,0:T(8,128)} %bitcast.85), custom_call_target="tpu_custom_call" | custom-call | tf_op jit(solution)/shard_map/pallas_call | solution.py:238
  285.6 0.7 slice_bitcast_fusion.7
  286.9 0.8 broadcast_select_fusion.4
  287.6 0.7 fusion.1
  288.9 4.3 %collective-permute-done.7 = f32[12,12,32]{2,1,0:T(8,128)S(1)} collective-permute-done((f32[12,12,32]{2,1,0:T(8,128)S(1)}, f32[12,12,32]{2,1,0:T(8,128)S(1)}, u32[]{:S(2)}, u32[]{:S(2)}) %collective-permute-start.7) | collective-permute-done | bytes 18464 | tf_op jit(solution)/shard_map/ppermute | solution.py:304
  293.2 0.7 broadcast_select_fusion.1
  294.1 1.4 select_select_fusion.entry_ref
  295.5 13.3 %shard_map.42 = f32[5,12,32,1440]{3,2,1,0:T(8,128)} custom-call(f32[5,12,32,1440]{3,2,1,0:T(8,128)} %get-tuple-element.22.state_ref, f32[12,32,1440]{2,1,0:T(8,128)S(1)} %copy-done, f32[12,32,1440]{2,1,0:T(8,128)S(1)} %copy-done.2, f32[5,12,32,128]{3,2,1,0:T(8,128)S(1)} %select_select_fusion.entry_ref), custom_call_target="tpu_custom_call" | custom-call | tf_op jit(solution)/shard_map/pallas_call | solution.py:288
  (79 shorter events, 8.8 us)
Async XLA Ops:
  2.8 15.2 %collective-permute-start = (f32[4,5,12,32]{3,0,2,1:T(4,128)S(1)}, f32[4,5,12,32]{3,0,2,1:T(4,128)S(1)}, u32[]{:S(2)}, u32[]{:S(2)}) collective-permute-start(f32[4,5,12,32]{3,0,2,1:T(4,128)S(1)} %pad_maximum_fusion.10), channel_id=1, source_target_pairs={{0,16},{16,0},{1,17},{17,1},{2,18},{18,2},{3,19},{19,3},{4,20},{20... | collective-permute-start | bytes 92168 | tf_op jit(solution)/shard_map/ppermute | solution.py:304
  9.2 13.7 %collective-permute-start.1 = (f32[4,2,32,1440]{3,2,1,0:T(8,128)}, f32[4,2,32,1440]{3,2,1,0:T(8,128)S(1)}, u32[]{:S(2)}, u32[]{:S(2)}) collective-permute-start(f32[4,2,32,1440]{3,2,1,0:T(8,128)} %pad_maximum_fusion), channel_id=1, source_target_pairs={{0,1},{1,2},{2,3},{3,4},{4,5},{5,6},{6,7},{7,8},{8,9},{9,10},{10,1... | collective-permute-start | bytes 4423688 | tf_op jit(solution)/shard_map/ppermute | solution.py:304
  10.8 3.4 %copy-start.18 = (s32[64]{0:T(128)S(1)}, s32[64]{0:T(128)}, u32[]{:S(2)}) copy-start(s32[64]{0:T(128)} %param.5) | copy-start | bytes 772
  12.1 12.0 %collective-permute-start.2 = (f32[4,2,32,1440]{3,2,1,0:T(8,128)}, f32[4,2,32,1440]{3,2,1,0:T(8,128)}, u32[]{:S(2)}, u32[]{:S(2)}) collective-permute-start(f32[4,2,32,1440]{3,2,1,0:T(8,128)} %pad_maximum_fusion.1), channel_id=1, source_target_pairs={{1,0},{2,1},{3,2},{4,3},{5,4},{6,5},{7,6},{8,7},{9,8},{10,9},{11,1... | collective-permute-start | bytes 4423688 | tf_op jit(solution)/shard_map/ppermute | solution.py:304
  17.9 5.1 %copy-start.17 = (f32[128]{0:T(128)}, f32[128]{0:T(128)S(1)}, u32[]{:S(2)}) copy-start(f32[128]{0:T(128)S(1)} %pad.37.clone) | copy-start | bytes 1540
  23.0 1.1 copy-start.7
  24.1 1.4 copy-start.8
  105.5 36.7 %copy-start.3 = (f32[12,32,128]{2,1,0:T(8,128)}, f32[12,32,128]{2,1,0:T(8,128)S(1)}, u32[]{:S(2)}) copy-start(f32[12,32,128]{2,1,0:T(8,128)S(1)} %get-tuple-element.19) | copy-start | bytes 589828
  105.5 36.7 %copy-start.5 = (f32[12,32,128]{2,1,0:T(8,128)}, f32[12,32,128]{2,1,0:T(8,128)S(1)}, u32[]{:S(2)}) copy-start(f32[12,32,128]{2,1,0:T(8,128)S(1)} %get-tuple-element.20) | copy-start | bytes 589828
  105.5 34.8 %copy-start.16 = (pred[12]{0:T(512)(128)(4,1)S(1)}, pred[12]{0:T(512)(128)(4,1)}, u32[]{:S(2)}) copy-start(pred[12]{0:T(512)(128)(4,1)} %broadcast_compare_fusion) | copy-start | bytes 40
  139.4 2.7 copy-start.13
  139.7 2.5 copy-start.14
  140.3 1.8 copy-start.11
  140.4 1.8 copy-start.12
  141.1 5.1 %collective-permute-start.3 = (f32[12,12,32]{2,1,0:T(8,128)}, f32[12,12,32]{2,1,0:T(8,128)}, u32[]{:S(2)}, u32[]{:S(2)}) collective-permute-start(f32[12,12,32]{2,1,0:T(8,128)} %fusion), channel_id=1, source_target_pairs={{0,16},{16,0},{1,17},{17,1},{2,18},{18,2},{3,19},{19,3},{4,20},{20... | collective-permute-start | bytes 55304 | tf_op jit(solution)/shard_map/ppermute | solution.py:304
  142.2 6.7 %copy-start = (f32[12,32,1440]{2,1,0:T(8,128)S(1)}, f32[12,32,1440]{2,1,0:T(8,128)}, u32[]{:S(2)}) copy-start(f32[12,32,1440]{2,1,0:T(8,128)} %get-tuple-element.16.scale_ref) | copy-start | bytes 6635524
  148.9 1.7 copy-start.1
  163.9 8.9 %copy-start.10 = (f32[5,12,32,1440]{3,2,1,0:T(8,128)S(1)}, f32[5,12,32,1440]{3,2,1,0:T(8,128)}, u32[]{:S(2)}) copy-start(f32[5,12,32,1440]{3,2,1,0:T(8,128)} %shard_map.39.state_ref) | copy-start | bytes 33177604
  167.4 24.3 %collective-permute-start.5 = (f32[4,2,32,1440]{3,2,1,0:T(8,128)}, f32[4,2,32,1440]{3,2,1,0:T(8,128)}, u32[]{:S(2)}, u32[]{:S(2)}) collective-permute-start(f32[4,2,32,1440]{3,2,1,0:T(8,128)} %pad_maximum_fusion.2), channel_id=1, source_target_pairs={{0,1},{1,2},{2,3},{3,4},{4,5},{5,6},{6,7},{7,8},{8,9},{9,10},{10,1... | collective-permute-start | bytes 4423688 | tf_op jit(solution)/shard_map/ppermute | solution.py:304
  171.4 20.2 %collective-permute-start.6 = (f32[4,2,32,1440]{3,2,1,0:T(8,128)}, f32[4,2,32,1440]{3,2,1,0:T(8,128)}, u32[]{:S(2)}, u32[]{:S(2)}) collective-permute-start(f32[4,2,32,1440]{3,2,1,0:T(8,128)} %pad_maximum_fusion.3), channel_id=1, source_target_pairs={{1,0},{2,1},{3,2},{4,3},{5,4},{6,5},{7,6},{8,7},{9,8},{10,9},{11,1... | collective-permute-start | bytes 4423688 | tf_op jit(solution)/shard_map/ppermute | solution.py:304
  178.3 6.1 %collective-permute-start.4 = (f32[4,5,12,32]{3,0,2,1:T(4,128)S(1)}, f32[4,5,12,32]{3,0,2,1:T(4,128)S(1)}, u32[]{:S(2)}, u32[]{:S(2)}) collective-permute-start(f32[4,5,12,32]{3,0,2,1:T(4,128)S(1)} %pad_maximum_fusion.11), channel_id=1, source_target_pairs={{0,16},{16,0},{1,17},{17,1},{2,18},{18,2},{3,19},{19,3},{4,20},{20... | collective-permute-start | bytes 92168 | tf_op jit(solution)/shard_map/ppermute | solution.py:304
  178.9 10.7 %slice-start = ((f32[5,12,32,1440]{3,2,1,0:T(8,128)}), f32[5,12,32,32]{3,2,1,0:T(8,128)S(1)}, s32[]{:S(2)}) async-start(f32[5,12,32,1440]{3,2,1,0:T(8,128)} %shard_map.39.state_ref), calls=%async_computation | async-start | bytes 1966080 | tf_op jit(solution)/shard_map/slice | solution.py:386
  262.0 0.7 copy-start.9
  262.7 31.4 %copy-start.4 = (f32[12,32,128]{2,1,0:T(8,128)S(1)}, f32[12,32,128]{2,1,0:T(8,128)}, u32[]{:S(2)}) copy-start(f32[12,32,128]{2,1,0:T(8,128)} %copy-done.3) | copy-start | bytes 589828
  262.7 31.4 %copy-start.15 = (f32[12]{0:T(128)S(1)}, f32[12]{0:T(128)}, u32[]{:S(2)}) copy-start(f32[12]{0:T(128)} %broadcast_multiply_fusion.2) | copy-start | bytes 148
  285.5 8.5 %copy-start.6 = (f32[12,32,128]{2,1,0:T(8,128)S(1)}, f32[12,32,128]{2,1,0:T(8,128)}, u32[]{:S(2)}) copy-start(f32[12,32,128]{2,1,0:T(8,128)} %copy-done.5) | copy-start | bytes 589828
  288.4 7.1 %copy-start.2 = (f32[12,32,1440]{2,1,0:T(8,128)S(1)}, f32[12,32,1440]{2,1,0:T(8,128)}, u32[]{:S(2)}) copy-start(f32[12,32,1440]{2,1,0:T(8,128)} %get-tuple-element.17.ones_ref) | copy-start | bytes 6635524
  288.4 4.9 %collective-permute-start.7 = (f32[12,12,32]{2,1,0:T(8,128)S(1)}, f32[12,12,32]{2,1,0:T(8,128)S(1)}, u32[]{:S(2)}, u32[]{:S(2)}) collective-permute-start(f32[12,12,32]{2,1,0:T(8,128)S(1)} %fusion.1), channel_id=1, source_target_pairs={{0,16},{16,0},{1,17},{17,1},{2,18},{18,2},{3,19},{19,3},{4,20},{20... | collective-permute-start | bytes 55304 | tf_op jit(solution)/shard_map/ppermute | solution.py:304

commit v3 on v2

--- a/solution.py
+++ b/solution.py
@@ -10,6 +10,7 @@
 SUBSTEPS = 2
 LANES = 128
 LEVELS = 8
+EDGE = 2
 
 time_step = 0.2
 coriolis = 0.5
@@ -30,12 +31,17 @@
     return scale, offsets
 
 
-def rates_kernel(first, band_ref, tab_ref, state_ref, tail_ref, south_ref, north_ref,
+def rates_kernel(first, inner, band_ref, tab_ref, state_ref, tail_ref,
                  decay_ref, decay_tail_ref, *refs):
+    refs = list(refs)
+    if not inner:
+        south_ref, north_ref = refs.pop(0), refs.pop(0)
+    out_ref, prefix_ref = refs.pop(0), refs.pop(0)
+    if not inner:
+        sums_ref = refs.pop(0)
     if first:
-        out_ref, prefix_ref, sums_ref, scale_ref, ones_ref, prefix_scale_ref, prefix_ones_ref, prod = refs
-    else:
-        out_ref, prefix_ref, sums_ref, prod = refs
+        scale_ref, ones_ref, prefix_scale_ref, prefix_ones_ref = refs[:4]
+    prod = refs[-1]
     rows = state_ref.shape[1]
     cols = state_ref.shape[3]
     main = cols // LANES * LANES
@@ -45,8 +51,8 @@
     wide_lane = lax.broadcasted_iota(jnp.int32, (LEVELS, width), 1)
     chunk_steps = max(1, (chunks - 1).bit_length())
 
-    for part in range(4):
-        for k in range(2):
+    for part in range(0 if inner else 4):
+        for k in range(EDGE):
             prod[part, k, :, :cols] = south_ref[part, k]
             prod[part, rows + 2 + k, :, :cols] = north_ref[part, k]
 
@@ -59,13 +65,19 @@
         prod[3, r + 2, :, :cols] = state_ref[4, r] * merid
         return carry
 
-    lax.fori_loop(0, rows, products, 0)
+    if inner:
+        lax.fori_loop(0, rows, products, 0)
+    else:
+        lax.fori_loop(0, 2 * EDGE, products, 0)
+        lax.fori_loop(rows - 2 * EDGE, rows, products, 0)
 
     def put(ref, index, value):
         ref[index + (slice(None), slice(0, main))] = value[:, :main]
         ref[index + (slice(None), slice(main, cols))] = value[:, main:cols]
 
-    def row(r, carry):
+    def row(i, carry):
+        r = i + EDGE if inner else jnp.where(i < EDGE, i, i + (rows - 2 * EDGE))
+
         def wide(f):
             return jnp.concatenate([state_ref[f, r, :, :main], tail_ref[f, r]], axis=1)
 
@@ -103,19 +115,20 @@
                     total = total + rates[f][:, k * LANES:(k + 1) * LANES]
                 sums_ref[f, side] = total
 
-        pl.when(r == 0)(lambda: put_sums(0))
-        pl.when(r == rows - 1)(lambda: put_sums(1))
+        if not inner:
+            pl.when(r == 0)(lambda: put_sums(0))
+            pl.when(r == rows - 1)(lambda: put_sums(1))
         in_band = band_ref[r] > 0
         state = [thick, zonal, merid, heat, tracer]
 
         @pl.when(jnp.logical_not(in_band))
         def _():
             for f in range(5):
-                put(out_ref, (f, r), state[f] + time_step * rates[f])
+                put(out_ref, (f, i), state[f] + time_step * rates[f])
             if first:
                 zero = jnp.zeros((LEVELS, width), jnp.float32)
-                put(scale_ref, (r,), zero)
-                put(ones_ref, (r,), zero)
+                put(scale_ref, (i,), zero)
+                put(ones_ref, (i,), zero)
 
         @pl.when(in_band)
         def _():
@@ -142,46 +155,60 @@
                 n = end - low
                 for f in range(5):
                     value = state[f][:, low:high] + amount * offsets[f]
-                    out_ref[f, r, :, low:end] = value[:, :n]
+                    out_ref[f, i, :, low:end] = value[:, :n]
                 if first:
-                    scale_ref[r, :, low:end] = scale[:, :n]
-                    ones_ref[r, :, low:end] = (time_step - amount * offsets[5])[:, :n]
+                    scale_ref[i, :, low:end] = scale[:, :n]
+                    ones_ref[i, :, low:end] = (time_step - amount * offsets[5])[:, :n]
             whole_scale, whole = lane_scan(whole_scale, whole, lane, chunk_steps)
             start = lane == 0
             before = [jnp.where(start, 0.0, pltpu.roll(w, 1, axis=1)) for w in whole]
             for f in range(5):
-                prefix_ref[f, r] = before[f]
+                prefix_ref[f, i] = before[f]
             if first:
-                prefix_scale_ref[r] = jnp.where(start, 1.0, pltpu.roll(whole_scale, 1, axis=1))
-                prefix_ones_ref[r] = before[5]
+                prefix_scale_ref[i] = jnp.where(start, 1.0, pltpu.roll(whole_scale, 1, axis=1))
+                prefix_ones_ref[i] = before[5]
 
         return carry
 
-    lax.fori_loop(0, rows, row, 0)
-
-
-def apply_kernel(state_ref, scale_ref, ones_ref, entry_ref, out_ref):
-    rows = state_ref.shape[1]
+    lax.fori_loop(0, rows - 2 * EDGE if inner else 2 * EDGE, row, 0)
+
+
+def apply_kernel(state_ref, scale_ref, ones_ref, edge_state_ref, edge_scale_ref, edge_ones_ref,
+                 entry_ref, out_ref):
+    rows = out_ref.shape[1]
+    inner = (state_ref, scale_ref, ones_ref)
+    edges = (edge_state_ref, edge_scale_ref, edge_ones_ref)
+    lax.fori_loop(
+        0, rows - 2 * EDGE, functools.partial(apply_row, *inner, entry_ref, out_ref, EDGE), 0
+    )
+    lax.fori_loop(0, EDGE, functools.partial(apply_row, *edges, entry_ref, out_ref, 0), 0)
+    lax.fori_loop(
+        EDGE,
+        2 * EDGE,
+        functools.partial(apply_row, *edges, entry_ref, out_ref, rows - 2 * EDGE),
+        0,
+    )
+
+
+def apply_row(state_ref, scale_ref, ones_ref, entry_ref, out_ref, shift_by, i, carry):
     cols = state_ref.shape[3]
     main = cols // LANES * LANES
     chunks = main // LANES + 1
 
-    def row(r, carry):
-        for f in range(5):
-            entry = entry_ref[f, r]
-            panel = jnp.broadcast_to(entry[:, LANES - 1:], (LEVELS, LANES))
-            for k in range(chunks):
-                low = k * LANES
-                end = min(low + LANES, cols)
-                inflow = jnp.broadcast_to(entry[:, k:k + 1], (LEVELS, LANES))
-                out_ref[f, r, :, low:end] = (
-                    state_ref[f, r, :, low:end]
-                    + scale_ref[r, :, low:end] * inflow[:, :end - low]
-                    + ones_ref[r, :, low:end] * panel[:, :end - low]
-                )
-        return carry
-
-    lax.fori_loop(0, rows, row, 0)
+    r = i + shift_by
+    for f in range(5):
+        entry = entry_ref[f, r]
+        panel = jnp.broadcast_to(entry[:, LANES - 1:], (LEVELS, LANES))
+        for k in range(chunks):
+            low = k * LANES
+            end = min(low + LANES, cols)
+            inflow = jnp.broadcast_to(entry[:, k:k + 1], (LEVELS, LANES))
+            out_ref[f, r, :, low:end] = (
+                state_ref[f, i, :, low:end]
+                + scale_ref[i, :, low:end] * inflow[:, :end - low]
+                + ones_ref[i, :, low:end] * panel[:, :end - low]
+            )
+    return carry
 
 
 def caps_kernel(caps_ref, out_ref, send_sem, recv_sem):
@@ -259,40 +286,52 @@
     return jax.ShapeDtypeStruct(shape, jnp.float32)
 
 
-def call_rates(first, band, table, state, tail, south, north, decay, decay_tail):
+def call_rates(first, band, table, state, tail, decay, decay_tail, halos=None):
     fields, rows, levels, cols = state.shape
     width = cols // LANES * LANES + LANES
-    outs = [
-        shaped(state.shape),
-        shaped((fields, rows, levels, LANES)),
-        shaped((fields, 2, levels, LANES)),
-    ]
+    inner = halos is None
+    count = rows - 2 * EDGE if inner else 2 * EDGE
+    outs = [shaped((fields, count, levels, cols)), shaped((fields, count, levels, LANES))]
+    if not inner:
+        outs += [shaped((fields, 2, levels, LANES))]
     if first:
-        outs += [shaped((rows, levels, cols))] * 2 + [shaped((rows, levels, LANES))] * 2
-    arrays = (state, tail, south, north, decay, decay_tail)
+        outs += [shaped((count, levels, cols))] * 2 + [shaped((count, levels, LANES))] * 2
+    arrays = (state, tail, decay, decay_tail) + (() if inner else halos)
     smem = pl.BlockSpec(memory_space=pltpu.SMEM)
+    cells = fields * count * levels * cols
     return pl.pallas_call(
-        functools.partial(rates_kernel, first),
+        functools.partial(rates_kernel, first, inner),
         grid=(levels // LEVELS,),
         in_specs=[smem, smem] + [level_block(x.shape) for x in arrays],
         out_specs=[level_block(x.shape) for x in outs],
         out_shape=outs,
         scratch_shapes=[pltpu.VMEM((4, rows + 4, LEVELS, width), jnp.float32)],
         compiler_params=pltpu.CompilerParams(vmem_limit_bytes=48 * 1024 * 1024),
+        cost_estimate=pl.CostEstimate(
+            flops=400 * cells, bytes_accessed=40 * cells, transcendentals=0
+        ),
     )(band, table, *arrays)
 
 
-def call_apply(state, scale, ones, entry):
-    levels = state.shape[2]
-    arrays = (state, scale, ones, entry)
+def call_apply(inner, edges, entry):
+    fields, rows, levels, _ = entry.shape
+    cols = inner[0].shape[3]
+    arrays = tuple(inner) + tuple(edges) + (entry,)
+    out = shaped((fields, rows, levels, cols))
     return pl.pallas_call(
         apply_kernel,
         grid=(levels // LEVELS,),
         in_specs=[level_block(x.shape) for x in arrays],
-        out_specs=level_block(state.shape),
-        out_shape=shaped(state.shape),
+        out_specs=level_block(out.shape),
+        out_shape=out,
         compiler_params=pltpu.CompilerParams(vmem_limit_bytes=48 * 1024 * 1024),
     )(*arrays)
+
+
+def join_rows(inner, edges, axis):
+    first = lax.slice_in_dim(edges, 0, EDGE, axis=axis)
+    last = lax.slice_in_dim(edges, EDGE, 2 * EDGE, axis=axis)
+    return jnp.concatenate([first, inner, last], axis=axis)
 
 
 def shift(x, axis, step, closed):
@@ -384,13 +423,15 @@
         south, north = lat_halos(state)
         west, east = lon_halos(state)
         tail = jnp.concatenate([state[..., main:], east, gap, west], axis=3)
-        outs = call_rates(
-            substep == 0, band, table, state, tail, south, north, decay, decay_tail
-        )
+        common = (substep == 0, band, table, state, tail, decay, decay_tail)
+        inner = list(call_rates(*common))
+        edges = list(call_rates(*common, halos=(south, north)))
+        sums = edges.pop(2)
+        prefix = join_rows(inner[1], edges[1], 1)
         if substep == 0:
-            partial, prefix, sums, scale, ones, prefix_scale, prefix_ones = outs
-        else:
-            partial, prefix, sums = outs
+            inner_maps, edge_maps = inner[2:4], edges[2:4]
+            prefix_scale = join_rows(inner[4], edges[4], 0)
+            prefix_ones = join_rows(inner[5], edges[5], 0)
         caps = share_caps(jnp.moveaxis(jnp.sum(sums, axis=-1), 1, 0))
         maps = jnp.concatenate(
             [
@@ -420,7 +461,7 @@
         )
         entry = jnp.where(lanes == LANES - 1, panel[..., None], entry)
         entry = jnp.where(in_band[:, None, None], entry, 0.0)
-        state = call_apply(partial, scale, ones, entry)
+        state = call_apply([inner[0]] + inner_maps, [edges[0]] + edge_maps, entry)
     return jnp.transpose(state, (0, 2, 1, 3))
 
 

time: 310 us -> 282 us (0.910)
  Pallas kernels: 230 us -> 201 us
  local copies, waits for them, and re-layouts: 27.5 us -> 34.9 us
  other arithmetic: 25.1 us -> 20.3 us
    pallas_call x2, Pallas kernels: 53.4 us -> 18.7 us  [share_caps(): pl.pallas_call(caps_kernel, out_shape=shaped(caps.shape), in_specs=[pl.Bl...]
    pallas_call x2 -> x4, Pallas kernels: 150 us -> 156 us  [call_rates(): pl.pallas_call(functools.partial(rates_kernel, first, inner), grid=(level...]
    slice x0 -> x4, local copies, waits for them, and re-layouts: none -> 3.59 us  [join_rows(): first = lax.slice_in_dim(edges, 0, EDGE, axis=axis)]
    unnamed x42 -> x56, local copies, waits for them, and re-layouts: 12.2 us -> 11.6 us
  transfers between devices with their start and end apart: 8 -> 8, of which waited for: 3 -> 3; matrix products, arithmetic and copies ran while one was open for 9% -> 9% of each run, Pallas kernels for 0% -> 36%
where the time goes in v3:
time: 282 us
  Pallas kernels  201 us (71%)
  local copies, waits for them, and re-layouts  34.9 us (12%)
  other arithmetic  20.3 us (7%)
  starting transfers between devices  12.7 us (5%)
  waiting for transfers between devices  12 us (4%)
    pallas_call x4, Pallas kernels, call_rates(): pl.pallas_call(functools.partial(rates_kernel, first, inner), grid=(level...  156 us
    pallas_call x2, Pallas kernels, call_apply(): pl.pallas_call(apply_kernel, grid=(levels // LEVELS,), in_specs=[level_bl...  26.5 us
    pallas_call x2, Pallas kernels, share_caps(): pl.pallas_call(caps_kernel, out_shape=shaped(caps.shape), in_specs=[pl.Bl...  18.7 us
    ppermute x8, starting transfers between devices, shift(): return lax.ppermute(x, axis, pairs)  12.7 us
    ppermute x8, waiting for transfers between devices, shift(): return lax.ppermute(x, axis, pairs)  12 us
    unnamed x56, local copies, waits for them, and re-layouts  11.6 us
    transpose x4, local copies, waits for them, and re-layouts, lon_halos(): head = jnp.moveaxis(state[..., :2], 3, 0)  7.08 us
  transfers between devices with their start and end apart: 8, of which 3 were waited for; matrix products, arithmetic and copies ran while one was open for 9% of the time, Pallas kernels for 36%

profile of v3, /device:TPU:0, one launch (start us, length us, event | category | flops | bytes accessed | tf_op | source)
XLA Modules:
  0.0 281.7 jit_solution(4053081312541823687)
XLA Ops:
  0.0 1.9 slice_bitcast_fusion.3
  2.8 3.0 %collective-permute-start = (f32[4,5,12,32]{3,0,2,1:T(4,128)S(1)}, f32[4,5,12,32]{3,0,2,1:T(4,128)}, u32[]{:S(2)}, u32[]{:S(2)}) collective-permute-start(f32[4,5,12,32]{3,0,2,1:T(4,128)S(1)} %pad_maximum_fusion.14), channel_id=1, source_target_pairs={{0,16},{16,0},{1,17},{17,1},{2,18},{18,2},{3,19},{19,3},{4,20},{20... | collective-permute-start | bytes 92168 | tf_op jit(solution)/shard_map/ppermute | solution.py:343
  5.9 2.1 fusion.13
  8.0 1.3 pad_maximum_fusion
  9.3 2.7 collective-permute-start.1
  12.0 1.3 pad_maximum_fusion.1
  13.3 1.3 collective-permute-start.2
  15.1 1.3 slice.278
  16.9 0.9 slice.283
  18.1 1.0 fusion.17
  20.5 53.8 %shard_map.37 = (f32[5,8,32,1440]{3,2,1,0:T(8,128)}, f32[5,8,32,128]{3,2,1,0:T(8,128)S(1)}, f32[8,32,1440]{2,1,0:T(8,128)S(1)}, f32[8,32,1440]{2,1,0:T(8,128)S(1...) custom-call(s32[12]{0:T(128)S(1)} %convert_element_type.30.band_ref, f32[12,8]{1,0:T(8,128)S(1)} %stack.50.tab_ref, ...), custom_call_target="tpu_custom_call" | custom-call | flops 737280000 | bytes 73728000 | tf_op jit(solution)/shard_map/pallas_call | solution.py:302
  74.3 0.9 copy-done.7
  76.5 29.2 %shard_map.38 = (f32[5,4,32,1440]{3,2,1,0:T(8,128)}, f32[5,4,32,128]{3,2,1,0:T(8,128)S(1)}, f32[5,2,32,128]{3,2,1,0:T(8,128)S(1)}, f32[4,32,1440]{2,1,0:T(8,128)...) custom-call(s32[12]{0:T(128)S(1)} %convert_element_type.30.band_ref, ...), custom_call_target="tpu_custom_call" | custom-call | flops 368640000 | bytes 36864000 | tf_op jit(solution)/shard_map/pallas_call | solution.py:302
  105.7 0.9 copy-done.1
  106.6 0.9 copy-done.4
  110.1 10.0 %shard_map.39 = f32[2,5,32]{2,1,0:T(8,128)} custom-call(f32[2,5,32]{2,1,0:T(8,128)} %bitcast.87), custom_call_target="tpu_custom_call" | custom-call | tf_op jit(solution)/shard_map/pallas_call | solution.py:265
  120.2 0.7 slice_bitcast_fusion.9
  120.9 0.8 fusion.18
  121.7 0.8 fusion.19
  122.5 1.0 fusion.15
  123.5 1.0 pad_maximum_fusion.8
  127.5 4.6 %collective-permute-done.3 = f32[12,12,32]{2,1,0:T(8,128)} collective-permute-done((f32[12,12,32]{2,1,0:T(8,128)}, f32[12,12,32]{2,1,0:T(8,128)}, u32[]{:S(2)}, u32[]{:S(2)}) %collective-permute-start.3) | collective-permute-done | bytes 18464 | tf_op jit(solution)/shard_map/ppermute | solution.py:343
  132.1 0.9 broadcast_select_fusion.3
  133.0 1.9 select_select_fusion.1.entry_ref
  135.0 13.2 %shard_map.40.state_ref = f32[5,12,32,1440]{3,2,1,0:T(8,128)} custom-call(f32[5,8,32,1440]{3,2,1,0:T(8,128)} %get-tuple-element.23.state_ref, f32[8,32,1440]{2,1,0:T(8,128)S(1)} %get-tuple-element.24.scale_ref, f32[8,32,1440]{2,1,0:T(8,128)S(1)} %get-tuple-element.25.ones_ref, f32[5,4,32,1440]{3,2,1,0:T(8,128)} %get-tuple-element.26.edge_state_ref, ...), custom_call_target="tpu_custom_call" | custom-call | tf_op jit(solution)/shard_map/pallas_call | solution.py:321
  148.2 2.1 fusion.12
  150.3 1.3 pad_maximum_fusion.2
  151.7 2.5 collective-permute-start.5
  154.2 1.2 pad_maximum_fusion.3
  155.4 1.5 collective-permute-start.6
  156.9 3.2 %slice_bitcast_fusion.1 = (f32[2,5,12,32]{0,3,2,1:T(8,128)}, f32[2,5,12,32]{0,3,2,1:T(8,128)}) fusion(f32[5,12,32,1440]{3,2,1,0:T(8,128)} %shard_map.40.state_ref), kind=kLoop, calls=%fused_computation.6 | loop fusion | bytes 61440 | tf_op jit(solution)/shard_map/transpose | solution.py:348
  160.1 1.6 copy.99
  161.7 1.6 copy.100
  164.0 2.3 slice.303
  166.3 3.1 %collective-permute-done.4 = f32[4,5,12,32]{3,0,2,1:T(4,128)S(1)} collective-permute-done((f32[4,5,12,32]{3,0,2,1:T(4,128)S(1)}, f32[4,5,12,32]{3,0,2,1:T(4,128)S(1)}, u32[]{:S(2)}, u32[]{:S(2)}) %collective-permute-start.4) | collective-permute-done | bytes 30752 | tf_op jit(solution)/shard_map/ppermute | solution.py:343
  169.4 1.4 copy.108
  170.8 1.4 copy.109
  172.2 2.5 pad_maximum_fusion.6.tail_ref
  174.7 47.3 %shard_map.41 = (f32[5,8,32,1440]{3,2,1,0:T(8,128)}, f32[5,8,32,128]{3,2,1,0:T(8,128)S(1)}) custom-call(s32[12]{0:T(128)S(1)} %convert_element_type.30.band_ref, f32[12,8]{1,0:T(8,128)S(1)} %stack.50.tab_ref, f32[5,12,32,1440]{3,2,1,0:T(8,128)} %shard_map.40.state_ref, f32[5,12,32,128]{3,2,1,0:T(8,128)S(1)} %pad_maximum_fusion.6.tail_ref, ...), custom_call_target="tpu_custom_call" | custom-call | flops 737280000 | bytes 73728000 | tf_op jit(solution)/shard_map/pallas_call | solution.py:302
  222.0 0.9 copy-done.9
  222.9 25.9 %shard_map.42 = (f32[5,4,32,1440]{3,2,1,0:T(8,128)}, f32[5,4,32,128]{3,2,1,0:T(8,128)S(1)}, f32[5,2,32,128]{3,2,1,0:T(8,128)S(1)}) custom-call(s32[12]{0:T(128)S(1)} %convert_element_type.30.band_ref, f32[12,8]{1,0:T(8,128)S(1)} %stack.50.tab_ref, f32[5,12,32,1440]{3,2,1,0:T(8,128)} %shard_map.40.state_ref, ...), custom_call_target="tpu_custom_call" | custom-call | flops 368640000 | bytes 36864000 | tf_op jit(solution)/shard_map/pallas_call | solution.py:302
  248.8 0.7 copy-done.12
  250.2 8.7 %shard_map.43 = f32[2,5,32]{2,1,0:T(8,128)} custom-call(f32[2,5,32]{2,1,0:T(8,128)} %bitcast.88), custom_call_target="tpu_custom_call" | custom-call | tf_op jit(solution)/shard_map/pallas_call | solution.py:265
  259.7 1.0 fusion.14
  260.7 1.2 pad_maximum_fusion.7
  263.2 4.3 %collective-permute-done.7 = f32[12,12,32]{2,1,0:T(8,128)S(1)} collective-permute-done((f32[12,12,32]{2,1,0:T(8,128)S(1)}, f32[12,12,32]{2,1,0:T(8,128)S(1)}, u32[]{:S(2)}, u32[]{:S(2)}) %collective-permute-start.7) | collective-permute-done | bytes 18464 | tf_op jit(solution)/shard_map/ppermute | solution.py:343
  267.7 0.8 select_select_fusion.entry_ref
  268.4 13.2 %shard_map.44 = f32[5,12,32,1440]{3,2,1,0:T(8,128)} custom-call(f32[5,8,32,1440]{3,2,1,0:T(8,128)} %get-tuple-element.36.state_ref, f32[8,32,1440]{2,1,0:T(8,128)S(1)} %get-tuple-element.24.scale_ref, f32[8,32,1440]{2,1,0:T(8,128)S(1)} %get-tuple-element.25.ones_ref, f32[5,4,32,1440]{3,2,1,0:T(8,128)} %get-tuple-element.37.edge_state_ref, ...), custom_call_target="tpu_custom_call" | custom-call | tf_op jit(solution)/shard_map/pallas_call | solution.py:321
  (102 shorter events, 13.9 us)
Async XLA Ops:
  2.8 15.2 %collective-permute-start = (f32[4,5,12,32]{3,0,2,1:T(4,128)S(1)}, f32[4,5,12,32]{3,0,2,1:T(4,128)}, u32[]{:S(2)}, u32[]{:S(2)}) collective-permute-start(f32[4,5,12,32]{3,0,2,1:T(4,128)S(1)} %pad_maximum_fusion.14), channel_id=1, source_target_pairs={{0,16},{16,0},{1,17},{17,1},{2,18},{18,2},{3,19},{19,3},{4,20},{20... | collective-permute-start | bytes 92168 | tf_op jit(solution)/shard_map/ppermute | solution.py:343
  9.3 67.3 %collective-permute-start.1 = (f32[4,2,32,1440]{3,2,1,0:T(8,128)}, f32[4,2,32,1440]{3,2,1,0:T(8,128)}, u32[]{:S(2)}, u32[]{:S(2)}) collective-permute-start(f32[4,2,32,1440]{3,2,1,0:T(8,128)} %pad_maximum_fusion), channel_id=1, source_target_pairs={{0,1},{1,2},{2,3},{3,4},{4,5},{5,6},{6,7},{7,8},{8,9},{9,10},{10,1... | collective-permute-start | bytes 4423688 | tf_op jit(solution)/shard_map/ppermute | solution.py:343
  12.0 2.8 %copy-start.25 = (s32[64]{0:T(128)S(1)}, s32[64]{0:T(128)}, u32[]{:S(2)}) copy-start(s32[64]{0:T(128)} %param.5) | copy-start | bytes 772
  13.3 63.2 %collective-permute-start.2 = (f32[4,2,32,1440]{3,2,1,0:T(8,128)}, f32[4,2,32,1440]{3,2,1,0:T(8,128)}, u32[]{:S(2)}, u32[]{:S(2)}) collective-permute-start(f32[4,2,32,1440]{3,2,1,0:T(8,128)} %pad_maximum_fusion.1), channel_id=1, source_target_pairs={{1,0},{2,1},{3,2},{4,3},{5,4},{6,5},{7,6},{8,7},{9,8},{10,9},{11,1... | collective-permute-start | bytes 4423688 | tf_op jit(solution)/shard_map/ppermute | solution.py:343
  74.3 0.9 copy-start.7
  75.2 0.7 copy-start.13
  75.9 0.7 copy-start.15
  105.7 0.9 copy-start.1
  106.6 0.9 copy-start.4
  107.5 0.7 copy-start.11
  108.2 0.6 copy-start.16
  108.8 0.6 copy-start.17
  109.5 15.2 %copy-start.14 = (f32[8,32,128]{2,1,0:T(8,128)S(1)}, f32[8,32,128]{2,1,0:T(8,128)}, u32[]{:S(2)}) copy-start(f32[8,32,128]{2,1,0:T(8,128)} %copy-done.13) | copy-start | bytes 393220
  120.1 5.3 %copy-start.8 = (f32[5,8,32,128]{3,2,1,0:T(8,128)S(1)}, f32[5,8,32,128]{3,2,1,0:T(8,128)}, u32[]{:S(2)}) copy-start(f32[5,8,32,128]{3,2,1,0:T(8,128)} %copy-done.7) | copy-start | bytes 1966084
  123.5 2.1 copy-start.22
  123.5 2.1 copy-start.23
  124.5 0.7 copy-start.18
  124.8 0.7 copy-start.20
  126.3 1.2 copy-start.24
  126.9 5.1 %collective-permute-start.3 = (f32[12,12,32]{2,1,0:T(8,128)}, f32[12,12,32]{2,1,0:T(8,128)}, u32[]{:S(2)}, u32[]{:S(2)}) collective-permute-start(f32[12,12,32]{2,1,0:T(8,128)} %fusion), channel_id=1, source_target_pairs={{0,16},{16,0},{1,17},{17,1},{2,18},{18,2},{3,19},{19,3},{4,20},{20... | collective-permute-start | bytes 55304 | tf_op jit(solution)/shard_map/ppermute | solution.py:343
  127.4 7.5 %copy-start.2 = (f32[4,32,1440]{2,1,0:T(8,128)S(1)}, f32[4,32,1440]{2,1,0:T(8,128)}, u32[]{:S(2)}) copy-start(f32[4,32,1440]{2,1,0:T(8,128)} %copy-done.1) | copy-start | bytes 2211844
  127.5 7.5 %copy-start.5 = (f32[4,32,1440]{2,1,0:T(8,128)S(1)}, f32[4,32,1440]{2,1,0:T(8,128)}, u32[]{:S(2)}) copy-start(f32[4,32,1440]{2,1,0:T(8,128)} %copy-done.4) | copy-start | bytes 2211844
  151.7 71.2 %collective-permute-start.5 = (f32[4,2,32,1440]{3,2,1,0:T(8,128)}, f32[4,2,32,1440]{3,2,1,0:T(8,128)}, u32[]{:S(2)}, u32[]{:S(2)}) collective-permute-start(f32[4,2,32,1440]{3,2,1,0:T(8,128)} %pad_maximum_fusion.2), channel_id=1, source_target_pairs={{0,1},{1,2},{2,3},{3,4},{4,5},{5,6},{6,7},{7,8},{8,9},{9,10},{10,1... | collective-permute-start | bytes 4423688 | tf_op jit(solution)/shard_map/ppermute | solution.py:343
  155.4 67.4 %collective-permute-start.6 = (f32[4,2,32,1440]{3,2,1,0:T(8,128)}, f32[4,2,32,1440]{3,2,1,0:T(8,128)}, u32[]{:S(2)}, u32[]{:S(2)}) collective-permute-start(f32[4,2,32,1440]{3,2,1,0:T(8,128)} %pad_maximum_fusion.3), channel_id=1, source_target_pairs={{1,0},{2,1},{3,2},{4,3},{5,4},{6,5},{7,6},{8,7},{9,8},{10,9},{11,1... | collective-permute-start | bytes 4423688 | tf_op jit(solution)/shard_map/ppermute | solution.py:343
  163.4 5.9 %collective-permute-start.4 = (f32[4,5,12,32]{3,0,2,1:T(4,128)S(1)}, f32[4,5,12,32]{3,0,2,1:T(4,128)S(1)}, u32[]{:S(2)}, u32[]{:S(2)}) collective-permute-start(f32[4,5,12,32]{3,0,2,1:T(4,128)S(1)} %pad_maximum_fusion.15), channel_id=1, source_target_pairs={{0,16},{16,0},{1,17},{17,1},{2,18},{18,2},{3,19},{19,3},{4,20},{20... | collective-permute-start | bytes 92168 | tf_op jit(solution)/shard_map/ppermute | solution.py:343
  172.2 2.6 copy-start
  222.0 0.9 copy-start.9
  248.8 0.7 copy-start.12
  260.7 6.9 %copy-start.10 = (f32[5,8,32,128]{3,2,1,0:T(8,128)S(1)}, f32[5,8,32,128]{3,2,1,0:T(8,128)}, u32[]{:S(2)}) copy-start(f32[5,8,32,128]{3,2,1,0:T(8,128)} %copy-done.9) | copy-start | bytes 1966084
  260.7 6.9 %copy-start.19 = (f32[12,32,128]{2,1,0:T(8,128)S(1)}, f32[12,32,128]{2,1,0:T(8,128)}, u32[]{:S(2)}) copy-start(f32[12,32,128]{2,1,0:T(8,128)} %copy-done.18) | copy-start | bytes 589828
  260.7 6.9 %copy-start.21 = (f32[12,32,128]{2,1,0:T(8,128)S(1)}, f32[12,32,128]{2,1,0:T(8,128)}, u32[]{:S(2)}) copy-start(f32[12,32,128]{2,1,0:T(8,128)} %copy-done.20) | copy-start | bytes 589828
  262.7 5.8 %copy-start.3 = (f32[4,32,1440]{2,1,0:T(8,128)S(1)}, f32[4,32,1440]{2,1,0:T(8,128)}, u32[]{:S(2)}) copy-start(f32[4,32,1440]{2,1,0:T(8,128)} %copy-done.1) | copy-start | bytes 2211844
  262.7 5.8 %copy-start.6 = (f32[4,32,1440]{2,1,0:T(8,128)S(1)}, f32[4,32,1440]{2,1,0:T(8,128)}, u32[]{:S(2)}) copy-start(f32[4,32,1440]{2,1,0:T(8,128)} %copy-done.4) | copy-start | bytes 2211844
  262.7 4.9 %collective-permute-start.7 = (f32[12,12,32]{2,1,0:T(8,128)S(1)}, f32[12,12,32]{2,1,0:T(8,128)S(1)}, u32[]{:S(2)}, u32[]{:S(2)}) collective-permute-start(f32[12,12,32]{2,1,0:T(8,128)S(1)} %fusion.1), channel_id=1, source_target_pairs={{0,16},{16,0},{1,17},{17,1},{2,18},{18,2},{3,19},{19,3},{4,20},{20... | collective-permute-start | bytes 55304 | tf_op jit(solution)/shard_map/ppermute | solution.py:343

commit v4 on v3

--- a/solution.py
+++ b/solution.py
@@ -82,9 +82,9 @@
             return jnp.concatenate([state_ref[f, r, :, :main], tail_ref[f, r]], axis=1)
 
         def slope(q):
-            near = pltpu.roll(q, width - 1, axis=1) - pltpu.roll(q, 1, axis=1)
-            far = pltpu.roll(q, width - 2, axis=1) - pltpu.roll(q, 2, axis=1)
-            return 8.0 * near - far
+            step = q - pltpu.roll(q, 2, axis=1)
+            next_steps = pltpu.roll(step, width - 1, axis=1), pltpu.roll(step, width - 2, axis=1)
+            return 8.0 * next_steps[0] - next_steps[1] - step
 
         lon_factor = tab_ref[r, 5]
         turn = tab_ref[r, 6]

time: 282 us -> 287 us (1.018)
  Pallas kernels: 201 us -> 207 us
    pallas_call x4, Pallas kernels: 156 us -> 162 us  [call_rates(): pl.pallas_call(functools.partial(rates_kernel, first, inner), grid=(level...]
  transfers between devices with their start and end apart: 8 -> 8, of which waited for: 3 -> 3; matrix products, arithmetic and copies ran while one was open for 9% -> 9% of each run, Pallas kernels for 36% -> 37%
where the time goes in v4:
time: 287 us; the launch traced here: 286 us
  Pallas kernels  207 us (72%)
  local copies, waits for them, and re-layouts  34.9 us (12%)
  other arithmetic  20.3 us (7%)
  starting transfers between devices  12.7 us (4%)
  waiting for transfers between devices  10.6 us (4%)
    pallas_call x4, Pallas kernels, call_rates(): pl.pallas_call(functools.partial(rates_kernel, first, inner), grid=(level...  162 us
    pallas_call x2, Pallas kernels, call_apply(): pl.pallas_call(apply_kernel, grid=(levels // LEVELS,), in_specs=[level_bl...  26.5 us
    pallas_call x2, Pallas kernels, share_caps(): pl.pallas_call(caps_kernel, out_shape=shaped(caps.shape), in_specs=[pl.Bl...  19.2 us
    ppermute x8, starting transfers between devices, shift(): return lax.ppermute(x, axis, pairs)  12.7 us
    unnamed x56, local copies, waits for them, and re-layouts  11.6 us
    ppermute x8, waiting for transfers between devices, shift(): return lax.ppermute(x, axis, pairs)  10.6 us
    transpose x4, local copies, waits for them, and re-layouts, lon_halos(): head = jnp.moveaxis(state[..., :2], 3, 0)  7.08 us
  transfers between devices with their start and end apart: 8, of which 3 were waited for; matrix products, arithmetic and copies ran while one was open for 9% of the time, Pallas kernels for 37%

profile of v4, /device:TPU:0, one launch (start us, length us, event | category | flops | bytes accessed | tf_op | source)
XLA Modules:
  0.0 286.4 jit_solution(9652861125954894734)
XLA Ops:
  0.0 1.9 slice_bitcast_fusion.3
  2.8 3.0 %collective-permute-start = (f32[4,5,12,32]{3,0,2,1:T(4,128)S(1)}, f32[4,5,12,32]{3,0,2,1:T(4,128)}, u32[]{:S(2)}, u32[]{:S(2)}) collective-permute-start(f32[4,5,12,32]{3,0,2,1:T(4,128)S(1)} %pad_maximum_fusion.14), channel_id=1, source_target_pairs={{0,16},{16,0},{1,17},{17,1},{2,18},{18,2},{3,19},{19,3},{4,20},{20... | collective-permute-start | bytes 92168 | tf_op jit(solution)/shard_map/ppermute | solution.py:343
  5.9 2.1 fusion.13
  8.0 1.3 pad_maximum_fusion
  9.3 2.7 collective-permute-start.1
  12.0 1.3 pad_maximum_fusion.1
  13.3 1.3 collective-permute-start.2
  15.1 1.3 slice.278
  16.9 0.9 slice.283
  18.1 1.0 fusion.17
  20.5 55.7 %shard_map.37 = (f32[5,8,32,1440]{3,2,1,0:T(8,128)}, f32[5,8,32,128]{3,2,1,0:T(8,128)S(1)}, f32[8,32,1440]{2,1,0:T(8,128)S(1)}, f32[8,32,1440]{2,1,0:T(8,128)S(1...) custom-call(s32[12]{0:T(128)S(1)} %convert_element_type.30.band_ref, f32[12,8]{1,0:T(8,128)S(1)} %stack.50.tab_ref, ...), custom_call_target="tpu_custom_call" | custom-call | flops 737280000 | bytes 73728000 | tf_op jit(solution)/shard_map/pallas_call | solution.py:302
  76.2 0.9 copy-done.7
  78.4 30.1 %shard_map.38 = (f32[5,4,32,1440]{3,2,1,0:T(8,128)}, f32[5,4,32,128]{3,2,1,0:T(8,128)S(1)}, f32[5,2,32,128]{3,2,1,0:T(8,128)S(1)}, f32[4,32,1440]{2,1,0:T(8,128)...) custom-call(s32[12]{0:T(128)S(1)} %convert_element_type.30.band_ref, ...), custom_call_target="tpu_custom_call" | custom-call | flops 368640000 | bytes 36864000 | tf_op jit(solution)/shard_map/pallas_call | solution.py:302
  108.5 0.9 copy-done.1
  109.4 0.9 copy-done.4
  110.3 0.7 copy-done.11
  113.0 9.1 %shard_map.39 = f32[2,5,32]{2,1,0:T(8,128)} custom-call(f32[2,5,32]{2,1,0:T(8,128)} %bitcast.87), custom_call_target="tpu_custom_call" | custom-call | tf_op jit(solution)/shard_map/pallas_call | solution.py:265
  122.1 0.7 slice_bitcast_fusion.9
  122.9 0.8 fusion.18
  123.6 0.8 fusion.19
  124.4 1.0 fusion.15
  125.5 1.0 pad_maximum_fusion.8
  129.4 4.4 %collective-permute-done.3 = f32[12,12,32]{2,1,0:T(8,128)} collective-permute-done((f32[12,12,32]{2,1,0:T(8,128)}, f32[12,12,32]{2,1,0:T(8,128)}, u32[]{:S(2)}, u32[]{:S(2)}) %collective-permute-start.3) | collective-permute-done | bytes 18464 | tf_op jit(solution)/shard_map/ppermute | solution.py:343
  133.8 0.9 broadcast_select_fusion.3
  134.8 1.9 select_select_fusion.1.entry_ref
  136.7 13.2 %shard_map.40.state_ref = f32[5,12,32,1440]{3,2,1,0:T(8,128)} custom-call(f32[5,8,32,1440]{3,2,1,0:T(8,128)} %get-tuple-element.23.state_ref, f32[8,32,1440]{2,1,0:T(8,128)S(1)} %get-tuple-element.24.scale_ref, f32[8,32,1440]{2,1,0:T(8,128)S(1)} %get-tuple-element.25.ones_ref, f32[5,4,32,1440]{3,2,1,0:T(8,128)} %get-tuple-element.26.edge_state_ref, ...), custom_call_target="tpu_custom_call" | custom-call | tf_op jit(solution)/shard_map/pallas_call | solution.py:321
  150.0 2.1 fusion.12
  152.1 1.3 pad_maximum_fusion.2
  153.4 2.5 collective-permute-start.5
  156.0 1.2 pad_maximum_fusion.3
  157.2 1.5 collective-permute-start.6
  158.7 3.2 %slice_bitcast_fusion.1 = (f32[2,5,12,32]{0,3,2,1:T(8,128)}, f32[2,5,12,32]{0,3,2,1:T(8,128)}) fusion(f32[5,12,32,1440]{3,2,1,0:T(8,128)} %shard_map.40.state_ref), kind=kLoop, calls=%fused_computation.6 | loop fusion | bytes 61440 | tf_op jit(solution)/shard_map/transpose | solution.py:348
  161.8 1.6 copy.99
  163.4 1.6 copy.100
  165.8 2.3 slice.303
  168.0 2.1 collective-permute-done.4
  170.2 1.4 copy.108
  171.5 1.4 copy.109
  172.9 2.5 pad_maximum_fusion.6.tail_ref
  175.5 49.2 %shard_map.41 = (f32[5,8,32,1440]{3,2,1,0:T(8,128)}, f32[5,8,32,128]{3,2,1,0:T(8,128)S(1)}) custom-call(s32[12]{0:T(128)S(1)} %convert_element_type.30.band_ref, f32[12,8]{1,0:T(8,128)S(1)} %stack.50.tab_ref, f32[5,12,32,1440]{3,2,1,0:T(8,128)} %shard_map.40.state_ref, f32[5,12,32,128]{3,2,1,0:T(8,128)S(1)} %pad_maximum_fusion.6.tail_ref, ...), custom_call_target="tpu_custom_call" | custom-call | flops 737280000 | bytes 73728000 | tf_op jit(solution)/shard_map/pallas_call | solution.py:302
  224.7 0.9 copy-done.9
  225.5 26.8 %shard_map.42 = (f32[5,4,32,1440]{3,2,1,0:T(8,128)}, f32[5,4,32,128]{3,2,1,0:T(8,128)S(1)}, f32[5,2,32,128]{3,2,1,0:T(8,128)S(1)}) custom-call(s32[12]{0:T(128)S(1)} %convert_element_type.30.band_ref, f32[12,8]{1,0:T(8,128)S(1)} %stack.50.tab_ref, f32[5,12,32,1440]{3,2,1,0:T(8,128)} %shard_map.40.state_ref, ...), custom_call_target="tpu_custom_call" | custom-call | flops 368640000 | bytes 36864000 | tf_op jit(solution)/shard_map/pallas_call | solution.py:302
  253.8 10.1 %shard_map.43 = f32[2,5,32]{2,1,0:T(8,128)} custom-call(f32[2,5,32]{2,1,0:T(8,128)} %bitcast.88), custom_call_target="tpu_custom_call" | custom-call | tf_op jit(solution)/shard_map/pallas_call | solution.py:265
  264.6 1.0 fusion.14
  265.6 1.2 pad_maximum_fusion.7
  268.2 4.1 %collective-permute-done.7 = f32[12,12,32]{2,1,0:T(8,128)S(1)} collective-permute-done((f32[12,12,32]{2,1,0:T(8,128)S(1)}, f32[12,12,32]{2,1,0:T(8,128)S(1)}, u32[]{:S(2)}, u32[]{:S(2)}) %collective-permute-start.7) | collective-permute-done | bytes 18464 | tf_op jit(solution)/shard_map/ppermute | solution.py:343
  272.4 0.8 select_select_fusion.entry_ref
  273.2 13.2 %shard_map.44 = f32[5,12,32,1440]{3,2,1,0:T(8,128)} custom-call(f32[5,8,32,1440]{3,2,1,0:T(8,128)} %get-tuple-element.36.state_ref, f32[8,32,1440]{2,1,0:T(8,128)S(1)} %get-tuple-element.24.scale_ref, f32[8,32,1440]{2,1,0:T(8,128)S(1)} %get-tuple-element.25.ones_ref, f32[5,4,32,1440]{3,2,1,0:T(8,128)} %get-tuple-element.37.edge_state_ref, ...), custom_call_target="tpu_custom_call" | custom-call | tf_op jit(solution)/shard_map/pallas_call | solution.py:321
  (102 shorter events, 13.9 us)
Async XLA Ops:
  2.8 15.2 %collective-permute-start = (f32[4,5,12,32]{3,0,2,1:T(4,128)S(1)}, f32[4,5,12,32]{3,0,2,1:T(4,128)}, u32[]{:S(2)}, u32[]{:S(2)}) collective-permute-start(f32[4,5,12,32]{3,0,2,1:T(4,128)S(1)} %pad_maximum_fusion.14), channel_id=1, source_target_pairs={{0,16},{16,0},{1,17},{17,1},{2,18},{18,2},{3,19},{19,3},{4,20},{20... | collective-permute-start | bytes 92168 | tf_op jit(solution)/shard_map/ppermute | solution.py:343
  9.3 69.2 %collective-permute-start.1 = (f32[4,2,32,1440]{3,2,1,0:T(8,128)}, f32[4,2,32,1440]{3,2,1,0:T(8,128)}, u32[]{:S(2)}, u32[]{:S(2)}) collective-permute-start(f32[4,2,32,1440]{3,2,1,0:T(8,128)} %pad_maximum_fusion), channel_id=1, source_target_pairs={{0,1},{1,2},{2,3},{3,4},{4,5},{5,6},{6,7},{7,8},{8,9},{9,10},{10,1... | collective-permute-start | bytes 4423688 | tf_op jit(solution)/shard_map/ppermute | solution.py:343
  12.0 2.8 copy-start.25
  13.3 65.1 %collective-permute-start.2 = (f32[4,2,32,1440]{3,2,1,0:T(8,128)}, f32[4,2,32,1440]{3,2,1,0:T(8,128)}, u32[]{:S(2)}, u32[]{:S(2)}) collective-permute-start(f32[4,2,32,1440]{3,2,1,0:T(8,128)} %pad_maximum_fusion.1), channel_id=1, source_target_pairs={{1,0},{2,1},{3,2},{4,3},{5,4},{6,5},{7,6},{8,7},{9,8},{10,9},{11,1... | collective-permute-start | bytes 4423688 | tf_op jit(solution)/shard_map/ppermute | solution.py:343
  76.2 0.9 copy-start.7
  77.1 0.7 copy-start.13
  77.8 0.7 copy-start.15
  108.5 0.9 copy-start.1
  109.4 0.9 copy-start.4
  110.3 0.7 copy-start.11
  111.0 0.6 copy-start.16
  111.6 0.6 copy-start.17
  112.3 14.4 %copy-start.14 = (f32[8,32,128]{2,1,0:T(8,128)S(1)}, f32[8,32,128]{2,1,0:T(8,128)}, u32[]{:S(2)}) copy-start(f32[8,32,128]{2,1,0:T(8,128)} %copy-done.13) | copy-start | bytes 393220
  122.1 5.3 %copy-start.8 = (f32[5,8,32,128]{3,2,1,0:T(8,128)S(1)}, f32[5,8,32,128]{3,2,1,0:T(8,128)}, u32[]{:S(2)}) copy-start(f32[5,8,32,128]{3,2,1,0:T(8,128)} %copy-done.7) | copy-start | bytes 1966084
  125.4 2.1 copy-start.22
  125.5 2.1 copy-start.23
  126.5 0.7 copy-start.18
  126.8 0.7 copy-start.20
  128.2 1.2 copy-start.24
  128.9 4.9 %collective-permute-start.3 = (f32[12,12,32]{2,1,0:T(8,128)}, f32[12,12,32]{2,1,0:T(8,128)}, u32[]{:S(2)}, u32[]{:S(2)}) collective-permute-start(f32[12,12,32]{2,1,0:T(8,128)} %fusion), channel_id=1, source_target_pairs={{0,16},{16,0},{1,17},{17,1},{2,18},{18,2},{3,19},{19,3},{4,20},{20... | collective-permute-start | bytes 55304 | tf_op jit(solution)/shard_map/ppermute | solution.py:343
  129.4 7.3 %copy-start.2 = (f32[4,32,1440]{2,1,0:T(8,128)S(1)}, f32[4,32,1440]{2,1,0:T(8,128)}, u32[]{:S(2)}) copy-start(f32[4,32,1440]{2,1,0:T(8,128)} %copy-done.1) | copy-start | bytes 2211844
  129.4 7.3 %copy-start.5 = (f32[4,32,1440]{2,1,0:T(8,128)S(1)}, f32[4,32,1440]{2,1,0:T(8,128)}, u32[]{:S(2)}) copy-start(f32[4,32,1440]{2,1,0:T(8,128)} %copy-done.4) | copy-start | bytes 2211844
  153.4 72.1 %collective-permute-start.5 = (f32[4,2,32,1440]{3,2,1,0:T(8,128)}, f32[4,2,32,1440]{3,2,1,0:T(8,128)}, u32[]{:S(2)}, u32[]{:S(2)}) collective-permute-start(f32[4,2,32,1440]{3,2,1,0:T(8,128)} %pad_maximum_fusion.2), channel_id=1, source_target_pairs={{0,1},{1,2},{2,3},{3,4},{4,5},{5,6},{6,7},{7,8},{8,9},{9,10},{10,1... | collective-permute-start | bytes 4423688 | tf_op jit(solution)/shard_map/ppermute | solution.py:343
  157.2 68.3 %collective-permute-start.6 = (f32[4,2,32,1440]{3,2,1,0:T(8,128)}, f32[4,2,32,1440]{3,2,1,0:T(8,128)}, u32[]{:S(2)}, u32[]{:S(2)}) collective-permute-start(f32[4,2,32,1440]{3,2,1,0:T(8,128)} %pad_maximum_fusion.3), channel_id=1, source_target_pairs={{1,0},{2,1},{3,2},{4,3},{5,4},{6,5},{7,6},{8,7},{9,8},{10,9},{11,1... | collective-permute-start | bytes 4423688 | tf_op jit(solution)/shard_map/ppermute | solution.py:343
  165.2 4.9 %collective-permute-start.4 = (f32[4,5,12,32]{3,0,2,1:T(4,128)S(1)}, f32[4,5,12,32]{3,0,2,1:T(4,128)S(1)}, u32[]{:S(2)}, u32[]{:S(2)}) collective-permute-start(f32[4,5,12,32]{3,0,2,1:T(4,128)S(1)} %pad_maximum_fusion.15), channel_id=1, source_target_pairs={{0,16},{16,0},{1,17},{17,1},{2,18},{18,2},{3,19},{19,3},{4,20},{20... | collective-permute-start | bytes 92168 | tf_op jit(solution)/shard_map/ppermute | solution.py:343
  172.9 2.6 copy-start
  224.7 0.9 copy-start.9
  252.3 0.7 copy-start.12
  265.6 6.8 %copy-start.10 = (f32[5,8,32,128]{3,2,1,0:T(8,128)S(1)}, f32[5,8,32,128]{3,2,1,0:T(8,128)}, u32[]{:S(2)}) copy-start(f32[5,8,32,128]{3,2,1,0:T(8,128)} %copy-done.9) | copy-start | bytes 1966084
  265.6 6.8 %copy-start.19 = (f32[12,32,128]{2,1,0:T(8,128)S(1)}, f32[12,32,128]{2,1,0:T(8,128)}, u32[]{:S(2)}) copy-start(f32[12,32,128]{2,1,0:T(8,128)} %copy-done.18) | copy-start | bytes 589828
  265.6 6.8 %copy-start.21 = (f32[12,32,128]{2,1,0:T(8,128)S(1)}, f32[12,32,128]{2,1,0:T(8,128)}, u32[]{:S(2)}) copy-start(f32[12,32,128]{2,1,0:T(8,128)} %copy-done.20) | copy-start | bytes 589828
  267.6 5.6 %copy-start.3 = (f32[4,32,1440]{2,1,0:T(8,128)S(1)}, f32[4,32,1440]{2,1,0:T(8,128)}, u32[]{:S(2)}) copy-start(f32[4,32,1440]{2,1,0:T(8,128)} %copy-done.1) | copy-start | bytes 2211844
  267.6 5.6 %copy-start.6 = (f32[4,32,1440]{2,1,0:T(8,128)S(1)}, f32[4,32,1440]{2,1,0:T(8,128)}, u32[]{:S(2)}) copy-start(f32[4,32,1440]{2,1,0:T(8,128)} %copy-done.4) | copy-start | bytes 2211844
  267.6 4.7 %collective-permute-start.7 = (f32[12,12,32]{2,1,0:T(8,128)S(1)}, f32[12,12,32]{2,1,0:T(8,128)S(1)}, u32[]{:S(2)}, u32[]{:S(2)}) collective-permute-start(f32[12,12,32]{2,1,0:T(8,128)S(1)} %fusion.1), channel_id=1, source_target_pairs={{0,16},{16,0},{1,17},{17,1},{2,18},{18,2},{3,19},{19,3},{4,20},{20... | collective-permute-start | bytes 55304 | tf_op jit(solution)/shard_map/ppermute | solution.py:343
